TPU v7x, 32 devices: a whole 2x2x4 slice. The times are simulated.
32 devices in a mesh: dp: 8 (over z, x), seq: 4 (over y, core).
Axes of the slice: x: 2, y: 2, z: 4, core: 2. Of those that a mesh axis runs over, the one named last changes fastest.
Arguments:
- block_input: bfloat16 [8, 592, 1024], P('dp', 'seq')
- key_mask: int32 [8, 592], P('dp', 'seq'), may hold values from 0 to 1, as said below
- valid: int32 [8], P('dp'), may hold values 0 or 1
- gains: bfloat16 [2, 2, 1024], P(None, None, 'dp'), may hold values from 0.5 to 1.5
- biases: bfloat16 [2, 6, 1024], P(None, None, 'dp'), may hold values from -1.1953125 to 1.1953125
- w_qkv: bfloat16 [2, 1024, 3072], P(None, 'dp'), may hold values from -0.1875 to 0.1875
- w_out: bfloat16 [2, 1024, 1024], P(None, 'dp'), may hold values from -1.5 to 1.5
- w_fc1: bfloat16 [2, 1024, 4096], P(None, 'dp'), may hold values from -0.1875 to 0.1875
- b_fc1: bfloat16 [2, 4096], P(None, 'dp'), may hold values from -1.1953125 to 1.1953125
- w_fc2: bfloat16 [2, 4096, 1024], P(None, 'dp'), may hold values from -0.09375 to 0.09375
- cotangent: bfloat16 [8, 592, 1024], P('dp', 'seq'), may hold values from -6 to 6
Outputs:
- block_output: bfloat16 [8, 592, 1024], P('dp', 'seq')
- grad_x: float32 [8, 592, 1024], P('dp', 'seq')
- rms: float32 [2, 3], replicated
- grad_gains: float32 [2, 2, 1024], P(None, None, 'dp')
- grad_biases: float32 [2, 5, 1024], P(None, None, 'dp')
- grad_query_bias: float32 [2, 1024], P(None, 'dp')
- grad_qkv: float32 [2, 1024, 3072], P(None, 'dp')
- grad_out: float32 [2, 1024, 1024], P(None, 'dp')
- grad_fc1: float32 [2, 1024, 4096], P(None, 'dp')
- grad_bfc1: float32 [2, 4096], P(None, 'dp')
- grad_fc2: float32 [2, 4096, 1024], P(None, 'dp')
Inputs may be any that keep to these rules, and one draw needn't show every extreme that they name: `key_mask`: position 0 of every image is 1 and positions 577 to 591 are 0.
All inputs are finite; a program needn't handle non-finite values. No bound on the sum of `valid` on one device may be relied on, other than what follows from the above.
Results may differ from a plain program's by a relative error of at most 0.015.
Values may be sent and summed in bfloat16 or wider, within the bound.
A program may use at most 320 MiB of HBM per device.

v0:
```python
from functools import partial
import math

import jax
import jax.numpy as jnp
from jax import lax
from jax.sharding import PartitionSpec as P

HEADS = 16
HEAD_DIM = 64


epsilon = 1e-05


def norm_parts(values_in, gain, shift):
    center = values_in - jnp.mean(values_in, -1, keepdims=True)
    inverse = lax.rsqrt(jnp.mean(center * center, -1, keepdims=True) + epsilon)
    normal = center * inverse
    return (normal * gain + shift, normal, inverse)


def norm_back(grad_output, normal, inverse, gain):
    grad_gain = jnp.sum(grad_output * normal, (0, 1))
    grad_shift = jnp.sum(grad_output, (0, 1))
    grad_norm = grad_output * gain
    plain_mean = jnp.mean(grad_norm, -1, keepdims=True)
    cross_mean = jnp.mean(grad_norm * normal, -1, keepdims=True)
    return (grad_gain, grad_shift, inverse * (grad_norm - plain_mean - normal * cross_mean))


def scores_of(query, keys, mask_row, score_scale):
    scores = (
        jnp.einsum("qhd,khd->hqk", query, keys, preferred_element_type=jnp.float32) * score_scale
    )
    return jnp.where(mask_row[None, None, :] > 0, scores, -1000000000.0)


def attend(score_scale, inputs):
    packed, mask_row = inputs
    query, keys, values_in = (packed[:, 0], packed[:, 1], packed[:, 2])
    scores = scores_of(query, keys, mask_row, score_scale)
    row_max = jnp.max(scores, -1, keepdims=True)
    log_total = row_max + jnp.log(jnp.sum(jnp.exp(scores - row_max), -1, keepdims=True))
    probs = jnp.exp(scores - log_total).astype(jnp.bfloat16)
    mixed = jnp.einsum("hqk,khd->qhd", probs, values_in, preferred_element_type=jnp.float32).astype(
        jnp.bfloat16
    )
    return (mixed, log_total[..., 0])


def attend_back(score_scale, inputs):
    packed, log_total, grad_mixed, mask_row = inputs
    query, keys, values_in = (packed[:, 0], packed[:, 1], packed[:, 2])
    scores = scores_of(query, keys, mask_row, score_scale)
    probs = jnp.exp(scores - log_total[..., None])
    grad_probs = jnp.einsum(
        "qhd,khd->hqk", grad_mixed, values_in, preferred_element_type=jnp.float32
    )
    inner = jnp.sum(probs * grad_probs, -1, keepdims=True)
    grad_scores = (probs * (grad_probs - inner)).astype(jnp.bfloat16)
    grad_query = (
        jnp.einsum("hqk,khd->qhd", grad_scores, keys, preferred_element_type=jnp.float32)
        * score_scale
    ).astype(jnp.bfloat16)
    grad_keys = (
        jnp.einsum("hqk,qhd->khd", grad_scores, query, preferred_element_type=jnp.float32)
        * score_scale
    ).astype(jnp.bfloat16)
    grad_values = jnp.einsum(
        "hqk,qhd->khd", probs.astype(jnp.bfloat16), grad_mixed, preferred_element_type=jnp.float32
    ).astype(jnp.bfloat16)
    return jnp.stack([grad_query, grad_keys, grad_values], 1)


def forward_layer(hidden, weights, full_mask, tok_valid, groups):
    w_qkv, w_out, w_fc1, w_fc2, gains, biases, b_fc1 = weights
    gains = gains.astype(jnp.float32)
    biases = biases.astype(jnp.float32)
    b_fc1 = b_fc1.astype(jnp.float32)
    images, local_rows, model_width = hidden.shape
    full_len = local_rows * groups
    per_group = HEADS // groups
    score_scale = 1.0 / math.sqrt(HEAD_DIM)
    normed, normal_one, inverse_one = norm_parts(hidden, gains[0], biases[0])
    normed_low = normed.astype(jnp.bfloat16)
    packed = jnp.einsum("isd,de->ise", normed_low, w_qkv, preferred_element_type=jnp.float32)
    packed = packed + jnp.concatenate([biases[1], jnp.zeros_like(biases[1]), biases[2]])
    packed = packed.astype(jnp.bfloat16).reshape(
        images, local_rows, 3, groups, model_width // groups
    )
    spread = lax.all_to_all(packed, "seq", split_axis=3, concat_axis=1, tiled=True)
    spread = spread.reshape(images, full_len, 3, per_group, HEAD_DIM)
    mixed, log_total = lax.map(partial(attend, score_scale), (spread, full_mask))
    mixed = mixed.reshape(images, full_len, 1, model_width // groups)
    mixed_tok = lax.all_to_all(mixed, "seq", split_axis=1, concat_axis=2, tiled=True).reshape(
        images, local_rows, model_width
    )
    branch = (
        jnp.einsum("isd,de->ise", mixed_tok, w_out, preferred_element_type=jnp.float32) + biases[3]
    )
    middle = hidden + branch
    normed_two, normal_two, inverse_two = norm_parts(middle, gains[1], biases[4])
    normed_two_low = normed_two.astype(jnp.bfloat16)
    inner = (
        jnp.einsum("isd,df->isf", normed_two_low, w_fc1, preferred_element_type=jnp.float32) + b_fc1
    )
    gate_sig = jax.nn.sigmoid(1.702 * inner)
    gated = (inner * gate_sig).astype(jnp.bfloat16)
    output = jnp.einsum("isf,fd->isd", gated, w_fc2, preferred_element_type=jnp.float32) + biases[5]
    result = middle + output
    layer_stat = jnp.stack(
        [
            jnp.sum(tok_valid * jnp.sum(hidden * hidden, -1)),
            jnp.sum(tok_valid * jnp.sum(branch * branch, -1)),
            jnp.sum(tok_valid * jnp.sum(output * output, -1)),
        ]
    )
    stored = (
        normal_one,
        inverse_one,
        normed_low,
        spread,
        log_total,
        mixed_tok,
        normal_two,
        inverse_two,
        normed_two_low,
        inner,
        gate_sig,
        gated,
    )
    return (result, stored, layer_stat)


def backward_layer(grad_result, weights, stored, full_mask, groups):
    w_qkv, w_out, w_fc1, w_fc2, gains, biases, b_fc1 = weights
    gains = gains.astype(jnp.float32)
    (
        normal_one,
        inverse_one,
        normed_low,
        spread,
        log_total,
        mixed_tok,
        normal_two,
        inverse_two,
        normed_two_low,
        inner,
        gate_sig,
        gated,
    ) = stored
    images, local_rows, model_width = grad_result.shape
    full_len = local_rows * groups
    per_group = HEADS // groups
    score_scale = 1.0 / math.sqrt(HEAD_DIM)
    grad_out_low = grad_result.astype(jnp.bfloat16)
    grad_bias_five = jnp.sum(grad_out_low.astype(jnp.float32), (0, 1))
    grad_fc2 = jnp.einsum("isf,isd->fd", gated, grad_out_low, preferred_element_type=jnp.float32)
    grad_gated = jnp.einsum("isd,fd->isf", grad_out_low, w_fc2, preferred_element_type=jnp.float32)
    grad_inner = (grad_gated * (gate_sig + 1.702 * inner * gate_sig * (1.0 - gate_sig))).astype(
        jnp.bfloat16
    )
    grad_bias_fc1 = jnp.sum(grad_inner.astype(jnp.float32), (0, 1))
    grad_fc1 = jnp.einsum(
        "isd,isf->df", normed_two_low, grad_inner, preferred_element_type=jnp.float32
    )
    grad_normed_two = jnp.einsum(
        "isf,df->isd", grad_inner, w_fc1, preferred_element_type=jnp.float32
    )
    grad_gain_two, grad_shift_two, grad_middle = norm_back(
        grad_normed_two, normal_two, inverse_two, gains[1]
    )
    grad_middle = grad_middle + grad_result
    grad_branch = grad_middle.astype(jnp.bfloat16)
    grad_bias_three = jnp.sum(grad_branch.astype(jnp.float32), (0, 1))
    grad_out_proj = jnp.einsum(
        "isd,ise->de", mixed_tok, grad_branch, preferred_element_type=jnp.float32
    )
    grad_mixed = jnp.einsum(
        "ise,de->isd", grad_branch, w_out, preferred_element_type=jnp.float32
    ).astype(jnp.bfloat16)
    grad_mixed = grad_mixed.reshape(images, local_rows, groups, model_width // groups)
    grad_heads = lax.all_to_all(grad_mixed, "seq", split_axis=2, concat_axis=1, tiled=True).reshape(
        images, full_len, per_group, HEAD_DIM
    )
    grad_packed = lax.map(
        partial(attend_back, score_scale), (spread, log_total, grad_heads, full_mask)
    )
    grad_packed = grad_packed.reshape(images, full_len, 3, 1, model_width // groups)
    grad_proj = lax.all_to_all(grad_packed, "seq", split_axis=1, concat_axis=3, tiled=True).reshape(
        images, local_rows, 3 * model_width
    )
    grad_bias_query = jnp.sum(grad_proj[..., :model_width].astype(jnp.float32), (0, 1))
    grad_bias_value = jnp.sum(grad_proj[..., 2 * model_width :].astype(jnp.float32), (0, 1))
    grad_proj_qkv = jnp.einsum(
        "isd,ise->de", normed_low, grad_proj, preferred_element_type=jnp.float32
    )
    grad_normed = jnp.einsum("ise,de->isd", grad_proj, w_qkv, preferred_element_type=jnp.float32)
    grad_gain_one, grad_shift_one, grad_hidden = norm_back(
        grad_normed, normal_one, inverse_one, gains[0]
    )
    grad_hidden = grad_hidden + grad_middle
    gain_grads = jnp.stack([grad_gain_one, grad_gain_two])
    bias_grads = jnp.stack(
        [
            grad_shift_one,
            grad_bias_query,
            grad_bias_value,
            grad_bias_three,
            grad_shift_two,
            grad_bias_five,
        ]
    )
    return (
        grad_hidden,
        (grad_proj_qkv, grad_out_proj, grad_fc1, grad_fc2, gain_grads, bias_grads, grad_bias_fc1),
    )


def local(
    block_input, key_mask, valid, gains, biases, w_qkv, w_out, w_fc1, b_fc1, w_fc2, cotangent
):
    layers = w_qkv.shape[0]
    groups = lax.axis_size("seq")
    model_width = block_input.shape[2]
    full_mask = lax.all_gather(key_mask, "seq", axis=1, tiled=True)
    tok_valid = (key_mask * valid[:, None]).astype(jnp.float32)
    token_count = jnp.sum(tok_valid)
    hidden = block_input.astype(jnp.float32)
    kept_weights = []
    stored_all = []
    stat_list = []
    for layer in range(layers):
        weights = (
            lax.all_gather(w_qkv[layer], "dp", axis=0, tiled=True),
            lax.all_gather(w_out[layer], "dp", axis=0, tiled=True),
            lax.all_gather(w_fc1[layer], "dp", axis=0, tiled=True),
            lax.all_gather(w_fc2[layer], "dp", axis=0, tiled=True),
            lax.all_gather(gains[layer], "dp", axis=1, tiled=True),
            lax.all_gather(biases[layer], "dp", axis=1, tiled=True),
            lax.all_gather(b_fc1[layer], "dp", axis=0, tiled=True),
        )
        hidden, stored, layer_stat = forward_layer(hidden, weights, full_mask, tok_valid, groups)
        kept_weights.append(weights)
        stored_all.append(stored)
        stat_list.append(layer_stat)
    stat_sums, count_all = lax.psum((jnp.stack(stat_list), token_count), ("dp", "seq"))
    rms = jnp.sqrt(stat_sums / (jnp.maximum(count_all, 1.0) * model_width))
    grad_hidden = cotangent.astype(jnp.float32) * tok_valid[..., None]
    shares_all = [None] * layers
    for layer in reversed(range(layers)):
        weights = (
            lax.all_gather(w_qkv[layer], "dp", axis=0, tiled=True),
            lax.all_gather(w_out[layer], "dp", axis=0, tiled=True),
            lax.all_gather(w_fc1[layer], "dp", axis=0, tiled=True),
            lax.all_gather(w_fc2[layer], "dp", axis=0, tiled=True),
            lax.all_gather(gains[layer], "dp", axis=1, tiled=True),
            lax.all_gather(biases[layer], "dp", axis=1, tiled=True),
            lax.all_gather(b_fc1[layer], "dp", axis=0, tiled=True),
        )
        grad_hidden, layer_grads = backward_layer(
            grad_hidden, weights, stored_all[layer], full_mask, groups
        )
        shares = (
            lax.psum_scatter(layer_grads[0], "dp", scatter_dimension=0, tiled=True),
            lax.psum_scatter(layer_grads[1], "dp", scatter_dimension=0, tiled=True),
            lax.psum_scatter(layer_grads[2], "dp", scatter_dimension=0, tiled=True),
            lax.psum_scatter(layer_grads[3], "dp", scatter_dimension=0, tiled=True),
            lax.psum_scatter(layer_grads[4], "dp", scatter_dimension=1, tiled=True),
            lax.psum_scatter(layer_grads[5], "dp", scatter_dimension=1, tiled=True),
            lax.psum_scatter(layer_grads[6], "dp", scatter_dimension=0, tiled=True),
        )
        shares_all[layer] = (
            lax.psum(shares[0].astype(jnp.bfloat16), "seq").astype(jnp.float32),
            lax.psum(shares[1].astype(jnp.bfloat16), "seq").astype(jnp.float32),
            lax.psum(shares[2].astype(jnp.bfloat16), "seq").astype(jnp.float32),
            lax.psum(shares[3].astype(jnp.bfloat16), "seq").astype(jnp.float32),
            lax.psum(shares[4].astype(jnp.bfloat16), "seq").astype(jnp.float32),
            lax.psum(shares[5].astype(jnp.bfloat16), "seq").astype(jnp.float32),
            lax.psum(shares[6].astype(jnp.bfloat16), "seq").astype(jnp.float32),
        )

    def stacked(position):
        return jnp.stack([shares_all[layer][position] for layer in range(layers)])

    bias_all = stacked(5)
    bias_rest = jnp.concatenate([bias_all[:, :1], bias_all[:, 2:]], 1)
    bias_query = bias_all[:, 1]
    return (
        hidden.astype(jnp.bfloat16),
        grad_hidden,
        rms,
        stacked(4),
        bias_rest,
        bias_query,
        stacked(0),
        stacked(1),
        stacked(2),
        stacked(6),
        stacked(3),
    )


def solution(mesh):
    return jax.shard_map(
        local,
        mesh=mesh,
        in_specs=(
            P("dp", "seq", None),
            P("dp", "seq"),
            P("dp"),
            P(None, None, "dp"),
            P(None, None, "dp"),
            P(None, "dp", None),
            P(None, "dp", None),
            P(None, "dp", None),
            P(None, "dp"),
            P(None, "dp", None),
            P("dp", "seq", None),
        ),
        out_specs=(
            P("dp", "seq", None),
            P("dp", "seq", None),
            P(),
            P(None, None, "dp"),
            P(None, None, "dp"),
            P(None, "dp"),
            P(None, "dp", None),
            P(None, "dp", None),
            P(None, "dp", None),
            P(None, "dp"),
            P(None, "dp", None),
        ),
        check_vma=False,
    )
```

profile of v0, /device:TPU:23, one launch (start us, length us, event | category | flops | bytes accessed | tf_op | source)
XLA Modules:
  0.0 2955.6 jit_solution(11511494019422866539)
XLA Ops:
  7.2 2.8 fusion.172
  12.6 3.0 fusion.171
  18.4 11.7 all-gather
  30.1 15.7 all-gather.8
  45.8 12.6 all-gather.1
  58.9 49.8 %all-gather.23.cloned.1.call-done = bf16[1,1024,3072]{2,1,0:T(8,128)(2,1)} async-done(((bf16[1,128,3072]{2,1,0:T(8,128)(2,1)}), bf16[1,1024,3072]{2,1,0:T(8,128)(2,1)}) %all-gather.23.cloned.1.call-update) | async-done | bytes 6291472 | tf_op jit(solution)/shard_map/all_gather | solution.py:236
  108.7 4.0 fusion.53
  114.3 4.7 all-to-all-start
  120.6 10.5 all-reduce
  145.7 5.2 all-to-all-start.1
  150.9 17.3 all-gather.5
  168.3 16.3 all-gather.7
  187.0 3.0 fusion.169
  190.2 95.1 %all-gather.27.cloned.1.call-done = bf16[1,1024,4096]{2,1,0:T(8,128)(2,1)} async-done(((bf16[1,128,4096]{2,1,0:T(8,128)(2,1)}), bf16[1,1024,4096]{2,1,0:T(8,128)(2,1)}) %all-gather.27.cloned.1.call-update) | async-done | bytes 8388624 | tf_op jit(solution)/shard_map/all_gather | solution.py:238
  285.4 6.4 fusion.30
  291.7 119.3 %all-gather.29.cloned.1.call-done = bf16[1,4096,1024]{2,1,0:T(8,128)(2,1)} async-done(((bf16[1,512,1024]{2,1,0:T(8,128)(2,1)}), bf16[1,4096,1024]{2,1,0:T(8,128)(2,1)}) %all-gather.29.cloned.1.call-update) | async-done | bytes 8388624 | tf_op jit(solution)/shard_map/all_gather | solution.py:239
  411.1 6.6 fusion.168
  417.9 92.4 %all-gather.31.cloned.1.call-done = bf16[1,1024,3072]{2,1,0:T(8,128)(2,1)} async-done(((bf16[1,128,3072]{2,1,0:T(8,128)(2,1)}), bf16[1,1024,3072]{2,1,0:T(8,128)(2,1)}) %all-gather.31.cloned.1.call-update) | async-done | bytes 6291472 | tf_op jit(solution)/shard_map/all_gather | solution.py:236
  510.3 4.0 fusion.50
  515.9 5.0 all-to-all-start.2
  521.5 10.7 all-to-all-done.2
  542.6 3.4 reduce.43
  546.8 5.2 all-to-all-start.3
  552.0 17.2 all-gather.12
  570.6 3.6 bitcast_reduce_fusion
  575.6 3.1 fusion.167
  579.7 106.3 %all-gather.35.cloned.1.call-done = bf16[1,1024,4096]{2,1,0:T(8,128)(2,1)} async-done(((bf16[1,128,4096]{2,1,0:T(8,128)(2,1)}), bf16[1,1024,4096]{2,1,0:T(8,128)(2,1)}) %all-gather.35.cloned.1.call-update) | async-done | bytes 8388624 | tf_op jit(solution)/shard_map/all_gather | solution.py:238
  686.0 6.6 fusion.33
  692.7 119.2 %all-gather.37.cloned.1.call-done = bf16[1,4096,1024]{2,1,0:T(8,128)(2,1)} async-done(((bf16[1,512,1024]{2,1,0:T(8,128)(2,1)}), bf16[1,4096,1024]{2,1,0:T(8,128)(2,1)}) %all-gather.37.cloned.1.call-update) | async-done | bytes 8388624 | tf_op jit(solution)/shard_map/all_gather | solution.py:239
  811.9 7.5 convert_reduce_fusion
  819.5 3.1 fusion.103
  824.1 2.9 convert_reduce_fusion.4
  835.4 8.7 all_to_all.120
  850.5 5.0 multiply_reduce_fusion.1
  866.5 18.8 all_to_all.121
  886.4 5.3 fusion.104
  893.6 6.9 convert_reduce_fusion.1
  900.6 3.1 fusion.105
  907.8 6.5 fusion.153
  914.3 2.8 fusion.82
  919.0 9.0 all_to_all.122
  934.5 5.0 multiply_reduce_fusion
  950.5 19.2 all_to_all.123
  970.7 6.4 fusion.147
  978.9 9.2 fusion.130
  989.6 8.2 fusion.150
  999.3 8.3 fusion.156
  1009.3 9.3 fusion.124
  1024.6 5.3 fusion.100
  1036.9 184.7 %reduce-scatter.23.cloned.1.call-done = f32[128,3072]{1,0:T(8,128)} async-done(((f32[1024,3072]{1,0:T(8,128)}), f32[128,3072]{1,0:T(8,128)}) %reduce-scatter.23.cloned.1.call-update) | async-done | bytes 1572880 | tf_op jit(solution)/shard_map/reduce_scatter | solution.py:266
  1224.0 207.5 %reduce-scatter.21.cloned.1.call-done = f32[128,3072]{1,0:T(8,128)} async-done(((f32[1024,3072]{1,0:T(8,128)}), f32[128,3072]{1,0:T(8,128)}) %reduce-scatter.21.cloned.1.call-update) | async-done | bytes 1572880 | tf_op jit(solution)/shard_map/reduce_scatter | solution.py:266
  1433.9 282.0 %reduce-scatter.35.cloned.1.call-done = f32[512,1024]{1,0:T(8,128)} async-done(((f32[4096,1024]{1,0:T(8,128)}), f32[512,1024]{1,0:T(8,128)}) %reduce-scatter.35.cloned.1.call-update) | async-done | bytes 2097168 | tf_op jit(solution)/shard_map/reduce_scatter | solution.py:269
  1718.6 283.1 %reduce-scatter.31.cloned.1.call-done = f32[128,4096]{1,0:T(8,128)} async-done(((f32[1024,4096]{1,0:T(8,128)}), f32[128,4096]{1,0:T(8,128)}) %reduce-scatter.31.cloned.1.call-update) | async-done | bytes 2097168 | tf_op jit(solution)/shard_map/reduce_scatter | solution.py:268
  2004.4 282.7 %reduce-scatter.29.cloned.1.call-done = f32[128,4096]{1,0:T(8,128)} async-done(((f32[1024,4096]{1,0:T(8,128)}), f32[128,4096]{1,0:T(8,128)}) %reduce-scatter.29.cloned.1.call-update) | async-done | bytes 2097168 | tf_op jit(solution)/shard_map/reduce_scatter | solution.py:268
  2289.7 283.0 %reduce-scatter.33.cloned.1.call-done = f32[512,1024]{1,0:T(8,128)} async-done(((f32[4096,1024]{1,0:T(8,128)}), f32[512,1024]{1,0:T(8,128)}) %reduce-scatter.33.cloned.1.call-update) | async-done | bytes 2097168 | tf_op jit(solution)/shard_map/reduce_scatter | solution.py:269
  2580.1 24.2 all-reduce.4
  2604.4 31.4 %reduce-scatter.39.cloned.1.call-done = f32[128,2]{1,0:T(8,128)} async-done(((f32[1024,2]{1,0:T(8,128)}), f32[128,2]{1,0:T(8,128)}) %reduce-scatter.39.cloned.1.call-update) | async-done | bytes 1040
  2636.8 54.8 %reduce-scatter.19.cloned.1.call-done = f32[6,128]{1,0:T(8,128)} async-done(((f32[6,1024]{1,0:T(8,128)}), f32[6,128]{1,0:T(8,128)}) %reduce-scatter.19.cloned.1.call-update) | async-done | bytes 3088 | tf_op jit(solution)/shard_map/reduce_scatter | solution.py:271
  2697.0 41.3 %all-reduce.3 = (f32[2,3]{1,0:T(2,128)S(1)}, f32[]{:T(128)}) all-reduce(f32[2,3]{1,0:T(2,128)S(1)} %pad_maximum_fusion.7, f32[]{:T(128)} %get-tuple-element.132), channel_id=1, replica_groups=mesh['dp'=8,'seq'=4] {'dp','seq'}, use_global_device_ids=true, to_apply=%region_34.35 | all-reduce | flops 7 | bytes 56 | tf_op jit(solution)/shard_map/psum | solution.py:248
  2741.2 15.3 reduce-scatter.37.cloned.1.call-done
  2757.4 54.4 %reduce-scatter.17.cloned.1.call-done = f32[6,128]{1,0:T(8,128)} async-done(((f32[6,1024]{1,0:T(8,128)}), f32[6,128]{1,0:T(8,128)}) %reduce-scatter.17.cloned.1.call-update) | async-done | bytes 3088 | tf_op jit(solution)/shard_map/reduce_scatter | solution.py:271
  2812.5 8.0 all-reduce.5
  2822.9 115.5 %all-reduce.9.cloned.1.call-done = (bf16[1,128,3072]{2,1,0:T(8,128)(2,1)}, bf16[1,128,3072]{2,1,0:T(8,128)(2,1)}, bf16[1,128,1024]{2,1,0:T(8,128)(2,1)}, bf16[1,...) async-done(((bf16[1,128,3072]{2,1,0:T(8,128)(2,1)}, ...) | async-done | bytes 6291472 | tf_op jit(solution)/shard_map/psum | solution.py:275
  2940.6 3.2 maximum_convert_fusion.2
  (346 shorter events, 154.4 us)
Async XLA Ops:
  7.2 3.9 copy-start.47
  7.2 101.5 %all-gather.23.cloned.1.call-start = ((), (), s32[]{:S(2)}) async-start(), calls=%async_computation.30 | async-start | bytes 7077888 | tf_op jit(solution)/shard_map/all_gather | solution.py:236
  10.1 176.9 %all-gather.25.cloned.1.call-start = ((), (), s32[]{:S(2)}) async-start(), calls=%async_computation.31 | async-start | bytes 2359296 | tf_op jit(solution)/shard_map/all_gather | solution.py:237
  11.0 274.3 %all-gather.27.cloned.1.call-start = ((), (), s32[]{:S(2)}) async-start(), calls=%async_computation.32 | async-start | bytes 9437184 | tf_op jit(solution)/shard_map/all_gather | solution.py:238
  12.6 398.5 %all-gather.29.cloned.1.call-start = ((), (), s32[]{:S(2)}) async-start(), calls=%async_computation.33 | async-start | bytes 9437184 | tf_op jit(solution)/shard_map/all_gather | solution.py:239
  15.6 14.4 copy-start.54
  15.6 42.8 %copy-start.27 = (bf16[1,148,1024]{2,1,0:T(8,128)(2,1)S(1)}, bf16[1,148,1024]{2,1,0:T(8,128)(2,1)}, u32[]{:S(2)}) copy-start(bf16[1,148,1024]{2,1,0:T(8,128)(2,1)} %param.11) | copy-start | bytes 909316
  15.7 494.7 %all-gather.31.cloned.1.call-start = ((), (), s32[]{:S(2)}) async-start(), calls=%async_computation.34 | async-start | bytes 7077888 | tf_op jit(solution)/shard_map/all_gather | solution.py:236
  16.3 559.3 %all-gather.33.cloned.1.call-start = ((), (), s32[]{:S(2)}) async-start(), calls=%async_computation.35 | async-start | bytes 2359296 | tf_op jit(solution)/shard_map/all_gather | solution.py:237
  16.8 669.2 %all-gather.35.cloned.1.call-start = ((), (), s32[]{:S(2)}) async-start(), calls=%async_computation.36 | async-start | bytes 9437184 | tf_op jit(solution)/shard_map/all_gather | solution.py:238
  17.6 794.3 %all-gather.37.cloned.1.call-start = ((), (), s32[]{:S(2)}) async-start(), calls=%async_computation.37 | async-start | bytes 9437184 | tf_op jit(solution)/shard_map/all_gather | solution.py:239
  112.7 6.4 copy-start.60
  112.7 7.6 copy-start.55
  112.7 18.4 copy-start.56
  114.3 16.8 all-to-all-start
  133.2 5.5 copy-start.21
  145.7 38.9 %all-to-all-start.1 = ((bf16[4,2,18944]{2,1,0:T(2,128)(2,1)}), bf16[4,2,18944]{2,1,0:T(2,128)(2,1)S(1)}, u32[]{:S(2)}, u32[]{:S(2)}) async-start(bf16[4,2,18944]{2,1,0:T(2,128)(2,1)} %reshape.578), calls=%async_computation.1 | async-start | bytes 606208 | tf_op jit(solution)/shard_map/all_to_all | solution.py:96
  186.9 104.8 %copy-start.39 = (bf16[19,8,4,256]{3,1,2,0:T(8,128)(2,1)}, bf16[19,8,4,256]{3,1,2,0:T(8,128)(2,1)S(1)}, u32[]{:S(2)}) copy-start(bf16[19,8,4,256]{3,1,2,0:T(8,128)(2,1)S(1)} %copy.115) | copy-start | bytes 933892
  190.0 221.1 %copy-start.7 = (f32[1,148,1024]{2,1,0:T(8,128)}, f32[1,148,1024]{2,1,0:T(8,128)S(1)}, u32[]{:S(2)}) copy-start(f32[1,148,1024]{2,1,0:T(8,128)S(1)} %get-tuple-element.168) | copy-start | bytes 1818628
  417.7 96.6 %copy-start.10 = (f32[1,148,1024]{2,1,0:T(8,128)}, f32[1,148,1024]{2,1,0:T(8,128)S(1)}, u32[]{:S(2)}) copy-start(f32[1,148,1024]{2,1,0:T(8,128)S(1)} %get-tuple-element.166) | copy-start | bytes 1818628
  515.9 16.4 all-to-all-start.2
  546.8 22.5 all-to-all-start.3
  552.0 481.3 %reduce-scatter.27.cloned.1.call-start = ((), (), s32[]{:S(2)}) async-start(), calls=%async_computation.25 | async-start | bytes 4718592 | tf_op jit(solution)/shard_map/reduce_scatter | solution.py:267
  811.9 7.5 copy-start.2
  811.9 7.5 copy-start.13
  819.4 3.2 copy-start.33
  819.5 3.3 copy-start.15
  819.5 3.3 copy-start.53
  819.5 4.6 copy-start.58
  830.6 204.4 %reduce-scatter.25.cloned.1.call-start = ((), (), s32[]{:S(2)}) async-start(), calls=%async_computation.24 | async-start | bytes 4718592 | tf_op jit(solution)/shard_map/reduce_scatter | solution.py:267
  848.3 7.3 slice-start.2
  850.5 5.1 slice-start.3
  855.6 3.5 copy-start.24
  860.1 4.3 copy-start.46
  885.8 5.9 copy-start.25
  886.4 5.5 copy-start.32
  891.7 8.8 slice-start.4
  892.2 11.7 copy-start.30
  893.6 6.9 slice-start.5
  893.6 6.9 copy-start.8
  907.7 313.8 %reduce-scatter.23.cloned.1.call-start = ((), (), s32[]{:S(2)}) async-start(), calls=%async_computation.23 | async-start | bytes 14155776 | tf_op jit(solution)/shard_map/reduce_scatter | solution.py:266
  914.3 16.2 copy-start.4
  914.3 517.2 %reduce-scatter.21.cloned.1.call-start = ((), (), s32[]{:S(2)}) async-start(), calls=%async_computation.22 | async-start | bytes 14155776 | tf_op jit(solution)/shard_map/reduce_scatter | solution.py:266
  932.3 7.2 slice-start
  934.5 5.0 slice-start.1
  939.5 3.5 copy-start.22
  944.1 4.3 copy-start.45
  970.7 6.5 copy-start.37
  977.2 738.7 %reduce-scatter.35.cloned.1.call-start = ((), (), s32[]{:S(2)}) async-start(), calls=%async_computation.29 | async-start | bytes 18874368 | tf_op jit(solution)/shard_map/reduce_scatter | solution.py:269
  988.1 1013.6 %reduce-scatter.31.cloned.1.call-start = ((), (), s32[]{:S(2)}) async-start(), calls=%async_computation.27 | async-start | bytes 18874368 | tf_op jit(solution)/shard_map/reduce_scatter | solution.py:268
  997.8 1289.2 %reduce-scatter.29.cloned.1.call-start = ((), (), s32[]{:S(2)}) async-start(), calls=%async_computation.26 | async-start | bytes 18874368 | tf_op jit(solution)/shard_map/reduce_scatter | solution.py:268
  1007.6 1565.2 %reduce-scatter.33.cloned.1.call-start = ((), (), s32[]{:S(2)}) async-start(), calls=%async_computation.28 | async-start | bytes 18874368 | tf_op jit(solution)/shard_map/reduce_scatter | solution.py:269
  1018.6 6.0 copy-start.29
  1018.6 6.0 copy-start.38
  1018.6 1617.3 %reduce-scatter.39.cloned.1.call-start = ((), (), s32[]{:S(2)}) async-start(), calls=%async_computation.39 | async-start | bytes 589824
  1022.3 1669.3 %reduce-scatter.19.cloned.1.call-start = ((), (), s32[]{:S(2)}) async-start(), calls=%async_computation.21 | async-start | bytes 36864 | tf_op jit(solution)/shard_map/reduce_scatter | solution.py:271
  1024.3 1732.2 %reduce-scatter.37.cloned.1.call-start = ((), (), s32[]{:S(2)}) async-start(), calls=%async_computation.38 | async-start | bytes 589824
  1032.4 1779.4 %reduce-scatter.17.cloned.1.call-start = ((), (), s32[]{:S(2)}) async-start(), calls=%async_computation.20 | async-start | bytes 36864 | tf_op jit(solution)/shard_map/reduce_scatter | solution.py:271
  1033.2 1905.2 %all-reduce.9.cloned.1.call-start = ((), (), s32[]{:S(2)}) async-start(), calls=%async_computation.40 | async-start | bytes 12582912 | tf_op jit(solution)/shard_map/psum | solution.py:275
  2575.5 3.2 copy-start.44
  2575.5 162.7 %copy-start.20 = (f32[1,148,1024]{2,1,0:T(8,128)S(1)}, f32[1,148,1024]{2,1,0:T(8,128)}, u32[]{:S(2)}) copy-start(f32[1,148,1024]{2,1,0:T(8,128)} %copy-done.19) | copy-start | bytes 1818628
  2575.5 162.7 %copy-start.43 = (f32[148,1024]{1,0:T(8,128)S(1)}, f32[148,1024]{1,0:T(8,128)}, u32[]{:S(2)}) copy-start(f32[148,1024]{1,0:T(8,128)} %copy-done.42) | copy-start | bytes 1818628
  2938.4 5.5 copy-start.50
  2938.4 5.5 copy-start.51
  (28 other events, 46.0 us)
Sparse Core Ops, SparseCore 0:
  10.2 98.3 all-gather.22
  111.4 47.9 all-gather.24
  162.1 123.2 all-gather.26
  287.9 123.1 all-gather.28
  413.1 97.1 all-gather.30
  512.3 47.7 all-gather.32
  562.8 123.1 all-gather.34
  688.7 123.1 all-gather.36
  830.8 88.2 reduce-scatter.26
  923.6 87.8 reduce-scatter.24
  1015.0 206.4 reduce-scatter.22
  1225.0 206.4 reduce-scatter.20
  1435.3 280.6 reduce-scatter.34
  1720.0 281.6 reduce-scatter.30
  2005.3 281.6 reduce-scatter.28
  2291.2 281.5 reduce-scatter.32
  2576.5 59.2 reduce-scatter.38
  2639.2 52.3 reduce-scatter.18
  2695.3 61.2 reduce-scatter.36
  2759.5 52.2 reduce-scatter.16
  2815.8 122.5 all-reduce.8
where the time goes:
time: 2960 us
  waiting for transfers between devices  2390 us (81%)
  blocking collectives  231 us (8%)
  matrix products  152 us (5%)
  local copies, waits for them, and re-layouts  78.6 us (3%)
  other arithmetic  63.9 us (2%)
    reduce_scatter x2, waiting for transfers between devices, local(): lax.psum_scatter(layer_grads[2], 'dp', scatter_dimension=0, tiled=True)  566 us
    reduce_scatter x2, waiting for transfers between devices, local(): lax.psum_scatter(layer_grads[3], 'dp', scatter_dimension=0, tiled=True)  565 us
    reduce_scatter x2, waiting for transfers between devices, local(): lax.psum_scatter(layer_grads[0], 'dp', scatter_dimension=0, tiled=True)  392 us
    all_gather x2, waiting for transfers between devices, local(): lax.all_gather(w_fc2[layer], 'dp', axis=0, tiled=True)  239 us
    all_gather x2, waiting for transfers between devices, local(): lax.all_gather(w_fc1[layer], 'dp', axis=0, tiled=True)  201 us
    all_gather x2, waiting for transfers between devices, local(): lax.all_gather(w_qkv[layer], 'dp', axis=0, tiled=True)  142 us
    psum x1, waiting for transfers between devices, local(): lax.psum(shares[0].astype(jnp.bfloat16), 'seq').astype(jnp.float32)  115 us
    reduce_scatter x2, waiting for transfers between devices, local(): lax.psum_scatter(layer_grads[5], 'dp', scatter_dimension=1, tiled=True)  109 us
  transfers between devices with their start and end apart: 25, of which 18 were waited for; matrix products, arithmetic and copies ran while one was open for 8% of the time, Pallas kernels for 0%

commit v1 on v0

v1 whole, which is shorter than its diff:
```python
from functools import partial
import math

import jax
import jax.numpy as jnp
from jax import lax
from jax.sharding import PartitionSpec as P

HEADS = 16
HEAD_DIM = 64
F32 = jnp.float32
BF16 = jnp.bfloat16

epsilon = 1e-05


def norm_parts(values_in, gain, shift):
    center = values_in - jnp.mean(values_in, -1, keepdims=True)
    inverse = lax.rsqrt(jnp.mean(center * center, -1, keepdims=True) + epsilon)
    normal = center * inverse
    return (normal * gain + shift, normal, inverse)


def norm_back(grad_output, normal, inverse, gain):
    grad_gain = jnp.sum(grad_output * normal, 0)
    grad_shift = jnp.sum(grad_output, 0)
    grad_norm = grad_output * gain
    plain_mean = jnp.mean(grad_norm, -1, keepdims=True)
    cross_mean = jnp.mean(grad_norm * normal, -1, keepdims=True)
    return (grad_gain, grad_shift, inverse * (grad_norm - plain_mean - normal * cross_mean))


def dot(a, b, ca=1, cb=0):
    return lax.dot_general(a, b, (((ca,), (cb,)), ((), ())), preferred_element_type=F32)


def split_heads(x, width):
    return x.reshape(x.shape[0], width // HEAD_DIM, HEAD_DIM)


def scores_of(query, keys, mask_row, scale):
    scores = jnp.einsum("qhd,khd->hqk", query, keys, preferred_element_type=F32) * scale
    return jnp.where(mask_row[None, None, :] > 0, scores, -1000000000.0)


def gather_rows(x):
    return lax.all_gather(x, "seq", axis=0, tiled=True)


def scatter_rows(x):
    return lax.psum_scatter(x.astype(BF16), "seq", scatter_dimension=0, tiled=True).astype(F32)


def forward_layer(hidden, weights, params, mask_row, tok_valid):
    w_qkv, w_out, w_fc1, w_fc2 = weights
    gains, biases, bias_q, bias_v, b_fc1 = params
    scale = 1.0 / math.sqrt(HEAD_DIM)
    width = w_out.shape[0]
    normed, normal_one, inverse_one = norm_parts(hidden, gains[0], biases[0])
    normed_all = gather_rows(normed.astype(BF16))
    packed = dot(normed_all, w_qkv)
    packed = (packed + jnp.concatenate([bias_q, jnp.zeros_like(bias_q), bias_v])).astype(BF16)
    query, keys, values = (split_heads(packed[:, i * width : (i + 1) * width], width) for i in range(3))
    scores = scores_of(query, keys, mask_row, scale)
    row_max = jnp.max(scores, -1, keepdims=True)
    log_total = row_max + jnp.log(jnp.sum(jnp.exp(scores - row_max), -1, keepdims=True))
    probs = jnp.exp(scores - log_total).astype(BF16)
    mixed = jnp.einsum("hqk,khd->qhd", probs, values, preferred_element_type=F32).astype(BF16)
    mixed = mixed.reshape(mixed.shape[0], width)
    branch = scatter_rows(dot(mixed, w_out)) + biases[3]
    middle = hidden + branch
    normed_two, normal_two, inverse_two = norm_parts(middle, gains[1], biases[4])
    normed_two_all = gather_rows(normed_two.astype(BF16))
    inner = dot(normed_two_all, w_fc1) + b_fc1
    gate_sig = jax.nn.sigmoid(1.702 * inner)
    gated = (inner * gate_sig).astype(BF16)
    output = scatter_rows(dot(gated, w_fc2)) + biases[5]
    stat = jnp.stack([jnp.sum(tok_valid * jnp.sum(v * v, -1)) for v in (hidden, branch, output)])
    stored = (normal_one, inverse_one, normed_all, query, keys, values, log_total, mixed,
              normal_two, inverse_two, normed_two_all, inner, gate_sig, gated)
    return (middle + output, stored, stat)


def backward_layer(grad_result, weights, params, stored, mask_row):
    w_qkv, w_out, w_fc1, w_fc2 = weights
    gains = params[0]
    scale = 1.0 / math.sqrt(HEAD_DIM)
    (normal_one, inverse_one, normed_all, query, keys, values, log_total, mixed,
     normal_two, inverse_two, normed_two_all, inner, gate_sig, gated) = stored
    out_low = grad_result.astype(BF16)
    grad_bias_five = jnp.sum(out_low.astype(F32), 0)
    out_all = gather_rows(out_low)
    grad_fc2 = dot(gated, out_all, 0, 0)
    grad_gated = dot(out_all, w_fc2, 1, 1)
    grad_inner = (grad_gated * (gate_sig + 1.702 * inner * gate_sig * (1.0 - gate_sig))).astype(BF16)
    grad_bias_fc1 = jnp.sum(grad_inner.astype(F32), 0)
    grad_fc1 = dot(normed_two_all, grad_inner, 0, 0)
    grad_normed_two = scatter_rows(dot(grad_inner, w_fc1, 1, 1))
    grad_gain_two, grad_shift_two, grad_middle = norm_back(grad_normed_two, normal_two, inverse_two, gains[1])
    grad_middle = grad_middle + grad_result
    branch_low = grad_middle.astype(BF16)
    grad_bias_three = jnp.sum(branch_low.astype(F32), 0)
    branch_all = gather_rows(branch_low)
    grad_out = dot(mixed, branch_all, 0, 0)
    width = w_out.shape[0]
    grad_mixed = split_heads(dot(branch_all, w_out, 1, 1).astype(BF16), width)
    scores = scores_of(query, keys, mask_row, scale)
    probs = jnp.exp(scores - log_total)
    grad_probs = jnp.einsum("qhd,khd->hqk", grad_mixed, values, preferred_element_type=F32)
    inner_sum = jnp.sum(probs * grad_probs, -1, keepdims=True)
    grad_scores = (probs * (grad_probs - inner_sum)).astype(BF16)
    grad_q = (jnp.einsum("hqk,khd->qhd", grad_scores, keys, preferred_element_type=F32) * scale).astype(BF16)
    grad_k = (jnp.einsum("hqk,qhd->khd", grad_scores, query, preferred_element_type=F32) * scale).astype(BF16)
    grad_v = jnp.einsum("hqk,qhd->khd", probs.astype(BF16), grad_mixed, preferred_element_type=F32).astype(BF16)
    rows = grad_q.shape[0]
    grad_proj = jnp.concatenate([g.reshape(rows, width) for g in (grad_q, grad_k, grad_v)], 1)
    grad_bias_proj = jnp.sum(grad_proj.astype(F32), 0)
    grad_qkv = dot(normed_all, grad_proj, 0, 0)
    grad_normed = scatter_rows(dot(grad_proj, w_qkv, 1, 1))
    grad_gain_one, grad_shift_one, grad_hidden = norm_back(grad_normed, normal_one, inverse_one, gains[0])
    grad_hidden = grad_hidden + grad_middle
    rows_sum = jnp.stack([grad_gain_one, grad_gain_two, grad_shift_one, grad_bias_three, grad_shift_two, grad_bias_five])
    return (grad_hidden, (grad_qkv, grad_out, grad_fc1, grad_fc2), rows_sum, grad_bias_proj, grad_bias_fc1)


def local(block_input, key_mask, valid, gains, biases, w_qkv, w_out, w_fc1, b_fc1, w_fc2, cotangent):
    layers = w_qkv.shape[0]
    groups = lax.axis_size("seq")
    shards = lax.axis_size("dp")
    me = lax.axis_index("seq")
    width = block_input.shape[2]
    hidden_width = w_fc2.shape[1] * shards
    part = width // groups
    images = block_input.shape[0]
    assert images == 1
    mask_row = lax.all_gather(key_mask, "seq", axis=1, tiled=True)[0]
    tok_valid = (key_mask * valid[:, None]).astype(F32)[0]
    hidden = block_input[0].astype(F32)
    small = jnp.concatenate([gains.reshape(layers, -1), biases.reshape(layers, -1), b_fc1], 1)
    small = lax.all_gather(small, "dp", axis=0).astype(F32)
    n_g, n_b = gains.shape[1] * gains.shape[2], biases.shape[1] * biases.shape[2]
    gains_all = small[:, :, :n_g].reshape(shards, layers, 2, -1).transpose(1, 2, 0, 3).reshape(layers, 2, width)
    biases_all = small[:, :, n_g : n_g + n_b].reshape(shards, layers, 6, -1).transpose(1, 2, 0, 3).reshape(layers, 6, width)
    fc_all = small[:, :, n_g + n_b :].transpose(1, 0, 2).reshape(layers, shards, groups, -1)
    fc_mine = lax.dynamic_index_in_dim(fc_all, me, 2, False).reshape(layers, -1)
    proj_mine = lax.dynamic_index_in_dim(biases_all.reshape(layers, 6, groups, part), me, 2, False)

    def columns(w, outer):
        view = w.reshape(w.shape[0], outer, groups, -1)
        return lax.dynamic_index_in_dim(view, me, 2, False).reshape(w.shape[0], -1)

    def rows_of(w):
        view = w.reshape(groups, -1, w.shape[1])
        return lax.dynamic_index_in_dim(view, me, 0, False)

    def gather(w):
        return lax.all_gather(w, "dp", axis=0, tiled=True)

    weights, params, stored_all, stats = [], [], [], []
    for layer in range(layers):
        weights.append((
            gather(columns(w_qkv[layer], 3)),
            rows_of(gather(w_out[layer])),
            gather(columns(w_fc1[layer], shards)),
            gather(rows_of(w_fc2[layer])),
        ))
        params.append((gains_all[layer], biases_all[layer], proj_mine[layer, 1], proj_mine[layer, 2], fc_mine[layer]))
    for layer in range(layers):
        hidden, stored, stat = forward_layer(hidden, weights[layer], params[layer], mask_row, tok_valid)
        stored_all.append(stored)
        stats.append(stat)
    totals = lax.psum(jnp.concatenate([jnp.stack(stats).reshape(-1), jnp.sum(tok_valid)[None]]), ("dp", "seq"))
    rms = jnp.sqrt(totals[:-1].reshape(layers, 3) / (jnp.maximum(totals[-1], 1.0) * width))

    grad_hidden = cotangent[0].astype(F32) * tok_valid[:, None]
    big = [None] * layers
    sums = [None] * layers
    for layer in reversed(range(layers)):
        grad_hidden, grads, rows_sum, grad_proj, grad_fc = backward_layer(
            grad_hidden, weights[layer], params[layer], stored_all[layer], mask_row
        )
        g_qkv, g_out, g_fc1, g_fc2 = (g.astype(BF16) for g in grads)
        g_out = lax.all_to_all(g_out, "seq", split_axis=1, concat_axis=0, tiled=True)

        def reduce_(g):
            g = lax.psum_scatter(g, "dp", scatter_dimension=0, tiled=True)
            return lax.all_gather(g, "seq", axis=0)

        def join(g, outer):
            view = g.reshape(groups, g.shape[1], outer, -1)
            return view.transpose(1, 2, 0, 3).reshape(g.shape[1], -1)

        big[layer] = (
            join(reduce_(g_qkv), 3).astype(F32),
            join(reduce_(g_out), 1).astype(F32),
            join(reduce_(g_fc1), shards).astype(F32),
            reduce_(g_fc2).reshape(w_fc2.shape[1], -1).astype(F32),
        )
        proj = lax.dynamic_update_slice(jnp.zeros((3, groups, part), F32), grad_proj.reshape(3, 1, part), (0, me, 0))
        fc = lax.dynamic_update_slice(jnp.zeros((shards, groups, hidden_width // (shards * groups)), F32),
                                      grad_fc.reshape(shards, 1, -1), (0, me, 0))
        sums[layer] = jnp.concatenate([
            rows_sum.reshape(6, shards, -1).transpose(1, 0, 2).reshape(shards, -1),
            proj.reshape(3, shards, -1).transpose(1, 0, 2).reshape(shards, -1),
            fc.reshape(shards, -1),
        ], 1)
    flat = jnp.stack(sums, 1).astype(F32)
    flat = lax.psum(lax.psum_scatter(flat, "dp", scatter_dimension=0, tiled=True)[0], "seq")
    per = width // shards
    rows9 = flat[:, : 9 * per].reshape(layers, 9, per)
    grad_bfc1 = flat[:, 9 * per :]
    stack = lambda i: jnp.stack([b[i] for b in big])
    bias_rest = jnp.concatenate([rows9[:, 2:3], rows9[:, 8:9], rows9[:, 3:6]], 1)
    return (
        hidden.astype(BF16)[None],
        grad_hidden[None],
        rms,
        rows9[:, :2],
        bias_rest,
        rows9[:, 6],
        stack(0),
        stack(1),
        stack(2),
        grad_bfc1,
        stack(3),
    )


def solution(mesh):
    return jax.shard_map(
        local,
        mesh=mesh,
        in_specs=(
            P("dp", "seq", None),
            P("dp", "seq"),
            P("dp"),
            P(None, None, "dp"),
            P(None, None, "dp"),
            P(None, "dp", None),
            P(None, "dp", None),
            P(None, "dp", None),
            P(None, "dp"),
            P(None, "dp", None),
            P("dp", "seq", None),
        ),
        out_specs=(
            P("dp", "seq", None),
            P("dp", "seq", None),
            P(),
            P(None, None, "dp"),
            P(None, None, "dp"),
            P(None, "dp"),
            P(None, "dp", None),
            P(None, "dp", None),
            P(None, "dp", None),
            P(None, "dp"),
            P(None, "dp", None),
        ),
        check_vma=False,
    )
```

time: 2960 us -> 1520 us (0.51)
  waiting for transfers between devices: 2390 us -> 932 us
  matrix products: 152 us -> 110 us
  blocking collectives: 231 us -> 267 us
  local copies, waits for them, and re-layouts: 78.6 us -> 114 us
    reduce_scatter x10 -> x8, waiting for transfers between devices: 1630 us -> 425 us  [reduce_(): g = lax.psum_scatter(g, 'dp', scatter_dimension=0, tiled=True)]
    psum x1 -> x0, waiting for transfers between devices: 115 us -> none  [local(): lax.psum(shares[0].astype(jnp.bfloat16), 'seq').astype(jnp.float32)]
    all_gather x8 -> x20, waiting for transfers between devices: 582 us -> 473 us  [the longest x8 349 us: gather(): return lax.all_gather(w, 'dp', axis=0, tiled=True)]
    unnamed x2 -> x8, blocking collectives: 34.7 us -> 135 us
    dot_general x36, matrix products: 152 us -> 110 us  [the longest x24 84.4 us: dot(): lax.dot_general(a, b, (((ca,), (cb,)), ((), ())), preferred_element_type=...]
    unnamed x155 -> x183, local copies, waits for them, and re-layouts: 32.6 us -> 72.8 us
    all_gather x6 -> x5, blocking collectives: 90.8 us -> 58.6 us  [the longest x4 36.1 us: reduce_(): return lax.all_gather(g, 'seq', axis=0)]
    all_to_all x4 -> x2, blocking collectives: 55.7 us -> 24.8 us  [local(): lax.all_to_all(g_out, 'seq', split_axis=1, concat_axis=0, tiled=True)]
  transfers between devices with their start and end apart: 25 -> 37, of which waited for: 18 -> 33; matrix products, arithmetic and copies ran while one was open for 8% -> 14% of each run, Pallas kernels for 0% -> 0%
where the time goes in v1:
time: 1520 us; the launch traced here: 1510 us
  waiting for transfers between devices  932 us (61%)
  blocking collectives  267 us (18%)
  local copies, waits for them, and re-layouts  114 us (8%)
  matrix products  110 us (7%)
  other arithmetic  56.8 us (4%)
  between operations  18.6 us (1%)
    reduce_scatter x8, waiting for transfers between devices, reduce_(): g = lax.psum_scatter(g, 'dp', scatter_dimension=0, tiled=True)  425 us
    all_gather x8, waiting for transfers between devices, gather(): return lax.all_gather(w, 'dp', axis=0, tiled=True)  349 us
    unnamed x8, blocking collectives  135 us
    dot_general x24, matrix products, dot(): lax.dot_general(a, b, (((ca,), (cb,)), ((), ())), preferred_element_type=...  84.4 us
    all_gather x8, waiting for transfers between devices, gather_rows(): return lax.all_gather(x, 'seq', axis=0, tiled=True)  83.6 us
    unnamed x183, local copies, waits for them, and re-layouts  72.8 us
    all_gather x4, waiting for transfers between devices, reduce_(): return lax.all_gather(g, 'seq', axis=0)  41.1 us
    psum x1, blocking collectives, local(): lax.psum(jnp.concatenate([jnp.stack(stats).reshape(-1), jnp.sum(tok_valid...  38.6 us
  transfers between devices with their start and end apart: 37, of which 33 were waited for; matrix products, arithmetic and copies ran while one was open for 14% of the time, Pallas kernels for 0%

profile of v1, /device:TPU:23, one launch (start us, length us, event | category | flops | bytes accessed | tf_op | source)
XLA Modules:
  0.0 1510.9 jit_solution(626261906087211542)
XLA Ops:
  8.7 22.5 %all-gather.13 = bf16[8,2,1536]{2,1,0:T(2,128)(2,1)S(1)} all-gather(bf16[1,2,1536]{2,1,0:T(2,128)(2,1)S(1)} %maximum_bitcast_fusion), channel_id=2, replica_groups=mesh['dp'=8,'seq'=4] {'dp'}, dimensions={0}, use_global_device_ids=true | all-gather | bytes 55296 | tf_op jit(solution)/shard_map/all_gather | solution.py:140
  41.0 9.6 all-reduce
  51.2 11.6 all-gather.67.cloned.1.call-done
  64.2 44.8 %all-gather.43.cloned.1.call-done = bf16[1024,768]{0,1:T(8,128)(2,1)} async-done(((bf16[128,768]{0,1:T(8,128)(2,1)}), bf16[1024,768]{0,1:T(8,128)(2,1)}) %all-gather.43.cloned.1.call-update) | async-done | bytes 1572880 | tf_op jit(solution)/shard_map/all_gather | solution.py:157
  119.8 39.8 %all-gather.51.cloned.1.call-done = bf16[1,1024,1024]{2,1,0:T(8,128)(2,1)} async-done(((bf16[1,128,1024]{2,1,0:T(8,128)(2,1)}), bf16[1,1024,1024]{2,1,0:T(8,128)(2,1)}) %all-gather.51.cloned.1.call-update) | async-done | bytes 2097168 | tf_op jit(solution)/shard_map/all_gather | solution.py:157
  162.3 15.6 %fusion = bf16[152,1024]{1,0:T(8,128)(2,1)} fusion(bf16[592,1024]{1,0:T(8,128)(2,1)} %convolution_convert_fusion.9), kind=kCustom, calls=%all-reduce-scatter | all-reduce-scatter fusion | flops 622593 | bytes 1524224
  183.1 3.3 concatenate.38
  201.8 8.9 all-gather.69.cloned.1.call-done
  213.0 49.6 %all-gather.45.cloned.1.call-done = bf16[1024,1024]{0,1:T(8,128)(2,1)} async-done(((bf16[128,1024]{0,1:T(8,128)(2,1)}), bf16[1024,1024]{0,1:T(8,128)(2,1)}) %all-gather.45.cloned.1.call-update) | async-done | bytes 2097168 | tf_op jit(solution)/shard_map/all_gather | solution.py:157
  262.6 4.8 fusion.122
  267.5 45.4 %all-gather.53.cloned.1.call-done = bf16[1,1024,1024]{2,1,0:T(8,128)(2,1)} async-done(((bf16[1,128,1024]{2,1,0:T(8,128)(2,1)}), bf16[1,1024,1024]{2,1,0:T(8,128)(2,1)}) %all-gather.53.cloned.1.call-update) | async-done | bytes 2097168 | tf_op jit(solution)/shard_map/all_gather | solution.py:157
  312.9 4.8 fusion.20
  317.7 15.6 %fusion.1 = bf16[152,1024]{1,0:T(8,128)(2,1)} fusion(bf16[592,1024]{1,0:T(8,128)(2,1)} %fusion.20), kind=kCustom, calls=%all-reduce-scatter.1 | all-reduce-scatter fusion | flops 622593 | bytes 1524224
  338.5 3.3 concatenate.39
  353.6 11.9 all-gather.71.cloned.1.call-done
  367.7 43.9 %all-gather.47.cloned.1.call-done = bf16[1024,768]{0,1:T(8,128)(2,1)} async-done(((bf16[128,768]{0,1:T(8,128)(2,1)}), bf16[1024,768]{0,1:T(8,128)(2,1)}) %all-gather.47.cloned.1.call-update) | async-done | bytes 1572880 | tf_op jit(solution)/shard_map/all_gather | solution.py:157
  430.6 31.0 %all-gather.55.cloned.1.call-done = bf16[1,1024,1024]{2,1,0:T(8,128)(2,1)} async-done(((bf16[1,128,1024]{2,1,0:T(8,128)(2,1)}), bf16[1,1024,1024]{2,1,0:T(8,128)(2,1)}) %all-gather.55.cloned.1.call-update) | async-done | bytes 2097168 | tf_op jit(solution)/shard_map/all_gather | solution.py:157
  464.3 22.0 %fusion.2 = bf16[152,1024]{1,0:T(8,128)(2,1)} fusion(bf16[592,1024]{1,0:T(8,128)(2,1)} %convolution_convert_fusion.8), kind=kCustom, calls=%all-reduce-scatter.2 | all-reduce-scatter fusion | flops 622593 | bytes 1524224
  491.6 3.3 concatenate.40
  506.1 11.4 all-gather.73.cloned.1.call-done
  519.7 49.1 %all-gather.49.cloned.1.call-done = bf16[1024,1024]{0,1:T(8,128)(2,1)} async-done(((bf16[128,1024]{0,1:T(8,128)(2,1)}), bf16[1024,1024]{0,1:T(8,128)(2,1)}) %all-gather.49.cloned.1.call-update) | async-done | bytes 2097168 | tf_op jit(solution)/shard_map/all_gather | solution.py:157
  568.8 4.8 fusion.123
  573.6 45.0 %all-gather.57.cloned.1.call-done = bf16[1,1024,1024]{2,1,0:T(8,128)(2,1)} async-done(((bf16[1,128,1024]{2,1,0:T(8,128)(2,1)}), bf16[1,1024,1024]{2,1,0:T(8,128)(2,1)}) %all-gather.57.cloned.1.call-update) | async-done | bytes 2097168 | tf_op jit(solution)/shard_map/all_gather | solution.py:157
  618.6 5.0 convert_reduce_fusion
  627.2 15.6 %fusion.4 = bf16[152,1024]{1,0:T(8,128)(2,1)} fusion(bf16[592,1024]{1,0:T(8,128)(2,1)} %convolution_convert_fusion.7), kind=kCustom, calls=%all-reduce-scatter.4 | all-reduce-scatter fusion | flops 622593 | bytes 1524224
  648.0 3.3 concatenate.42
  656.3 19.6 %all-gather.77.cloned.1.call-done = bf16[4,148,1024]{2,1,0:T(8,128)(2,1)} async-done(((bf16[1,148,1024]{2,1,0:T(8,128)(2,1)}), bf16[4,148,1024]{2,1,0:T(8,128)(2,1)}) %all-gather.77.cloned.1.call-update) | async-done | bytes 1212432 | tf_op jit(solution)/shard_map/all_gather | solution.py:47
  685.9 4.9 multiply_reduce_fusion.1
  697.5 15.7 %fusion.5 = bf16[152,1024]{1,0:T(8,128)(2,1)} fusion(bf16[592,1024]{1,0:T(8,128)(2,1)} %convolution_convert_fusion.11), kind=kCustom, calls=%all-reduce-scatter.5 | all-reduce-scatter fusion | flops 622593 | bytes 1524224
  715.3 3.2 collective-permute-done.5
  718.5 3.3 concatenate.43
  726.8 20.3 %all-gather.79.cloned.1.call-done = bf16[4,148,1024]{2,1,0:T(8,128)(2,1)} async-done(((bf16[1,148,1024]{2,1,0:T(8,128)(2,1)}), bf16[4,148,1024]{2,1,0:T(8,128)(2,1)}) %all-gather.79.cloned.1.call-update) | async-done | bytes 1212432 | tf_op jit(solution)/shard_map/all_gather | solution.py:47
  749.3 5.0 convert_reduce_fusion.1
  757.8 15.9 %fusion.6 = bf16[152,1024]{1,0:T(8,128)(2,1)} fusion(bf16[592,1024]{1,0:T(8,128)(2,1)} %convolution_convert_fusion.6), kind=kCustom, calls=%all-reduce-scatter.6 | all-reduce-scatter fusion | flops 622593 | bytes 1524224
  778.9 3.3 concatenate.44
  787.3 4.8 convolution_convert_fusion.2
  792.2 4.8 convolution_convert_fusion.3
  799.1 12.4 all_to_all.38
  811.6 5.3 convolution_convert_fusion
  816.9 4.9 fusion.23
  822.2 4.1 convolution_convert_fusion.4
  836.0 5.0 multiply_reduce_fusion
  847.7 24.7 %fusion.102 = (bf16[152,1024]{1,0:T(8,128)(2,1)S(1)}, bf16[152,1024]{1,0:T(8,128)(2,1)S(1)}) fusion(bf16[592,1024]{1,0:T(8,128)(2,1)S(1)} %copy-done.43, bf16[592,1024]{1,0:T(8,128)(2,1)} %convolution_convert_fusion.10), kind=kCustom, calls=%all-reduce-scatter.8 | all-reduce-scatter fusion | flops 1245185 | bytes 3047936
  880.1 12.4 all_to_all.39
  892.7 5.3 convolution_convert_fusion.1
  901.9 45.6 %reduce-scatter.33.cloned.1.call-done = bf16[128,1024]{1,0:T(8,128)(2,1)} async-done(((bf16[1024,1024]{1,0:T(8,128)(2,1)}), bf16[128,1024]{1,0:T(8,128)(2,1)}) %reduce-scatter.33.cloned.1.call-update) | async-done | bytes 262160 | tf_op jit(solution)/shard_map/reduce_scatter | solution.py:186
  948.1 63.3 %reduce-scatter.31.cloned.1.call-done = bf16[128,256]{1,0:T(8,128)(2,1)} async-done(((bf16[1024,256]{1,0:T(8,128)(2,1)}), bf16[128,256]{1,0:T(8,128)(2,1)}) %reduce-scatter.31.cloned.1.call-update) | async-done | bytes 65552 | tf_op jit(solution)/shard_map/reduce_scatter | solution.py:186
  1011.4 8.4 all-gather.8
  1020.7 61.4 %reduce-scatter.39.cloned.1.call-done = bf16[128,1024]{1,0:T(8,128)(2,1)} async-done(((bf16[1024,1024]{1,0:T(8,128)(2,1)}), bf16[128,1024]{1,0:T(8,128)(2,1)}) %reduce-scatter.39.cloned.1.call-update) | async-done | bytes 262160 | tf_op jit(solution)/shard_map/reduce_scatter | solution.py:186
  1083.4 67.2 %reduce-scatter.27.cloned.1.call-done = bf16[128,768]{1,0:T(8,128)(2,1)} async-done(((bf16[1024,768]{1,0:T(8,128)(2,1)}), bf16[128,768]{1,0:T(8,128)(2,1)}) %reduce-scatter.27.cloned.1.call-update) | async-done | bytes 196624 | tf_op jit(solution)/shard_map/reduce_scatter | solution.py:186
  1150.7 9.5 all-gather.6
  1168.5 38.6 %psum.14 = f32[7]{0:T(128)S(1)} all-reduce(f32[7]{0:T(128)S(1)} %pad_maximum_fusion.9), channel_id=1, replica_groups=mesh['dp'=8,'seq'=4] {'dp','seq'}, use_global_device_ids=true, to_apply=%region_43.44 | all-reduce | flops 7 | bytes 56 | tf_op jit(solution)/shard_map/psum | solution.py:172
  1210.8 11.4 all-reduce.21.cloned.1.call-done
  1223.5 10.5 psum.15
  1236.4 5.7 all-gather.61.cloned.1.call-done
  1246.7 58.5 %reduce-scatter.29.cloned.1.call-done = bf16[128,256]{1,0:T(8,128)(2,1)} async-done(((bf16[1024,256]{1,0:T(8,128)(2,1)}), bf16[128,256]{1,0:T(8,128)(2,1)}) %reduce-scatter.29.cloned.1.call-update) | async-done | bytes 65552 | tf_op jit(solution)/shard_map/reduce_scatter | solution.py:186
  1305.2 8.4 all-gather.7
  1313.8 62.8 %reduce-scatter.37.cloned.1.call-done = bf16[128,1024]{1,0:T(8,128)(2,1)} async-done(((bf16[1024,1024]{1,0:T(8,128)(2,1)}), bf16[128,1024]{1,0:T(8,128)(2,1)}) %reduce-scatter.37.cloned.1.call-update) | async-done | bytes 262160 | tf_op jit(solution)/shard_map/reduce_scatter | solution.py:186
  1378.0 66.7 %reduce-scatter.25.cloned.1.call-done = bf16[128,768]{1,0:T(8,128)(2,1)} async-done(((bf16[1024,768]{1,0:T(8,128)(2,1)}), bf16[128,768]{1,0:T(8,128)(2,1)}) %reduce-scatter.25.cloned.1.call-update) | async-done | bytes 196624 | tf_op jit(solution)/shard_map/reduce_scatter | solution.py:186
  1444.7 9.7 all-gather.5
  1458.9 4.7 all-gather.59.cloned.1.call-done
  1469.6 12.3 all-gather.65.cloned.1.call-done
  1482.0 18.4 %all-gather.63.cloned.1.call-done = bf16[512,1024]{1,0:T(8,128)(2,1)} async-done(((bf16[128,1024]{1,0:T(8,128)(2,1)}), bf16[512,1024]{1,0:T(8,128)(2,1)}) %all-gather.63.cloned.1.call-update) | async-done | bytes 1048592 | tf_op jit(solution)/shard_map/all_gather | solution.py:187
  1500.4 3.8 maximum_convert_fusion.1
  (424 shorter events, 224.6 us)
Async XLA Ops:
  7.2 29.1 %copy-start.26 = (bf16[2,128,3072]{2,1,0:T(8,128)(2,1)S(1)}, bf16[2,128,3072]{2,1,0:T(8,128)(2,1)}, u32[]{:S(2)}) copy-start(bf16[2,128,3072]{2,1,0:T(8,128)(2,1)} %param.16) | copy-start | bytes 4718596
  7.2 55.6 %all-gather.67.cloned.1.call-start = ((), (), s32[]{:S(2)}) async-start(), calls=%async_computation.30 | async-start | bytes 1556480 | tf_op jit(solution)/shard_map/all_gather | solution.py:47
  36.2 72.7 %all-gather.43.cloned.1.call-start = ((), (), s32[]{:S(2)}) async-start(), calls=%async_computation.10 | async-start | bytes 1769472 | tf_op jit(solution)/shard_map/all_gather | solution.py:157
  38.4 121.2 %all-gather.51.cloned.1.call-start = ((), (), s32[]{:S(2)}) async-start(), calls=%async_computation.22 | async-start | bytes 2359296 | tf_op jit(solution)/shard_map/all_gather | solution.py:157
  39.3 171.4 %all-gather.69.cloned.1.call-start = ((), (), s32[]{:S(2)}) async-start(), calls=%async_computation.31 | async-start | bytes 1556480 | tf_op jit(solution)/shard_map/all_gather | solution.py:47
  64.2 44.8 %copy-start.41 = (bf16[592,1024]{1,0:T(8,128)(2,1)}, bf16[592,1024]{1,0:T(8,128)(2,1)S(1)}, u32[]{:S(2)}) copy-start(bf16[592,1024]{1,0:T(8,128)(2,1)S(1)} %reshape.541) | copy-start | bytes 3637252
  159.6 26.8 %copy-start.2 = (bf16[1,148,1024]{2,1,0:T(8,128)(2,1)S(1)}, bf16[1,148,1024]{2,1,0:T(8,128)(2,1)}, u32[]{:S(2)}) copy-start(bf16[1,148,1024]{2,1,0:T(8,128)(2,1)} %param.11) | copy-start | bytes 909316
  178.7 4.4 collective-permute-start
  188.9 5.1 copy-start.47
  190.9 71.7 %all-gather.45.cloned.1.call-start = ((), (), s32[]{:S(2)}) async-start(), calls=%async_computation.11 | async-start | bytes 2359296 | tf_op jit(solution)/shard_map/all_gather | solution.py:157
  198.0 114.9 %all-gather.53.cloned.1.call-start = ((), (), s32[]{:S(2)}) async-start(), calls=%async_computation.23 | async-start | bytes 2359296 | tf_op jit(solution)/shard_map/all_gather | solution.py:157
  201.5 164.0 %all-gather.71.cloned.1.call-start = ((), (), s32[]{:S(2)}) async-start(), calls=%async_computation.32 | async-start | bytes 1556480 | tf_op jit(solution)/shard_map/all_gather | solution.py:47
  201.8 547.5 %copy-start.50 = (f32[1,8,1,128]{3,2,0,1:T(1,128)}, f32[1,8,1,128]{3,2,0,1:T(1,128)S(1)}, u32[]{:S(2)}) copy-start(f32[1,8,1,128]{3,2,0,1:T(1,128)S(1)} %get-tuple-element.124) | copy-start | bytes 12292
  334.1 4.4 collective-permute-start.1
  343.9 7.2 copy-start.53
  345.6 66.0 %all-gather.47.cloned.1.call-start = ((), (), s32[]{:S(2)}) async-start(), calls=%async_computation.12 | async-start | bytes 1769472 | tf_op jit(solution)/shard_map/all_gather | solution.py:157
  348.0 63.7 %copy-start.54 = (f32[768]{0:T(1024)S(1)}, f32[768]{0:T(1024)}, u32[]{:S(2)}) copy-start(f32[768]{0:T(1024)} %get-tuple-element.136) | copy-start | bytes 9220
  349.6 112.0 %all-gather.55.cloned.1.call-start = ((), (), s32[]{:S(2)}) async-start(), calls=%async_computation.24 | async-start | bytes 2359296 | tf_op jit(solution)/shard_map/all_gather | solution.py:157
  350.4 153.5 %all-gather.75.cloned.1.call-start = ((), (), s32[]{:S(2)}) async-start(), calls=%async_computation.34 | async-start | bytes 1556480 | tf_op jit(solution)/shard_map/all_gather | solution.py:47
  353.6 163.9 %all-gather.73.cloned.1.call-start = ((), (), s32[]{:S(2)}) async-start(), calls=%async_computation.33 | async-start | bytes 1556480 | tf_op jit(solution)/shard_map/all_gather | solution.py:47
  487.0 4.5 collective-permute-start.2
  498.0 70.7 %all-gather.49.cloned.1.call-start = ((), (), s32[]{:S(2)}) async-start(), calls=%async_computation.13 | async-start | bytes 2359296 | tf_op jit(solution)/shard_map/all_gather | solution.py:157
  502.0 116.6 %all-gather.57.cloned.1.call-start = ((), (), s32[]{:S(2)}) async-start(), calls=%async_computation.25 | async-start | bytes 2359296 | tf_op jit(solution)/shard_map/all_gather | solution.py:157
  503.8 172.2 %all-gather.77.cloned.1.call-start = ((), (), s32[]{:S(2)}) async-start(), calls=%async_computation.35 | async-start | bytes 1556480 | tf_op jit(solution)/shard_map/all_gather | solution.py:47
  618.6 6.0 copy-start.57
  643.5 4.4 collective-permute-start.4
  656.1 90.9 %all-gather.79.cloned.1.call-start = ((), (), s32[]{:S(2)}) async-start(), calls=%async_computation.36 | async-start | bytes 1556480 | tf_op jit(solution)/shard_map/all_gather | solution.py:47
  682.8 8.1 slice-start.2
  685.9 8.6 copy-start.27
  714.0 4.5 collective-permute-start.5
  726.7 100.3 %all-gather.81.cloned.1.call-start = ((), (), s32[]{:S(2)}) async-start(), calls=%async_computation.37 | async-start | bytes 1556480 | tf_op jit(solution)/shard_map/all_gather | solution.py:47
  749.3 6.0 copy-start.56
  757.7 24.4 %copy-start.48 = (f32[148]{0:T(256)S(1)}, f32[148]{0:T(256)}, u32[]{:S(2)}) copy-start(f32[148]{0:T(256)} %copy-done.47) | copy-start | bytes 1780
  774.4 4.5 collective-permute-start.6
  787.2 91.5 %reduce-scatter.35.cloned.1.call-start = ((), (), s32[]{:S(2)}) async-start(), calls=%async_computation.19 | async-start | bytes 2359296 | tf_op jit(solution)/shard_map/reduce_scatter | solution.py:186
  792.1 155.4 %reduce-scatter.33.cloned.1.call-start = ((), (), s32[]{:S(2)}) async-start(), calls=%async_computation.18 | async-start | bytes 2359296 | tf_op jit(solution)/shard_map/reduce_scatter | solution.py:186
  797.0 214.4 %reduce-scatter.31.cloned.1.call-start = ((), (), s32[]{:S(2)}) async-start(), calls=%async_computation.17 | async-start | bytes 589824 | tf_op jit(solution)/shard_map/reduce_scatter | solution.py:186
  811.5 270.5 %reduce-scatter.39.cloned.1.call-start = ((), (), s32[]{:S(2)}) async-start(), calls=%async_computation.21 | async-start | bytes 2359296 | tf_op jit(solution)/shard_map/reduce_scatter | solution.py:186
  816.8 333.8 %reduce-scatter.27.cloned.1.call-start = ((), (), s32[]{:S(2)}) async-start(), calls=%async_computation.15 | async-start | bytes 1769472 | tf_op jit(solution)/shard_map/reduce_scatter | solution.py:186
  816.9 4.9 copy-start.28
  816.9 4.9 copy-start.30
  816.9 4.9 copy-start.32
  826.4 395.9 %all-reduce.21.cloned.1.call-start = ((), (), s32[]{:S(2)}) async-start(), calls=%async_computation.38 | async-start | bytes 212992
  833.8 7.2 slice-start
  836.0 8.7 copy-start.33
  836.0 5.0 slice-start.1
  847.7 26.2 %copy-start.34 = (bf16[4,64,592]{2,1,0:T(8,128)(2,1)S(1)}, bf16[4,64,592]{2,1,0:T(8,128)(2,1)}, u32[]{:S(2)}) copy-start(bf16[4,64,592]{2,1,0:T(8,128)(2,1)} %copy-done.33) | copy-start | bytes 909316
  847.7 26.2 %copy-start.37 = (bf16[4,64,592]{2,1,0:T(8,128)(2,1)S(1)}, bf16[4,64,592]{2,1,0:T(8,128)(2,1)}, u32[]{:S(2)}) copy-start(bf16[4,64,592]{2,1,0:T(8,128)(2,1)} %copy-done.36) | copy-start | bytes 909316
  872.4 7.1 copy-start.11
  872.4 7.1 copy-start.19
  872.4 4.5 collective-permute-start.7
  878.7 363.4 %all-gather.61.cloned.1.call-start = ((), (), s32[]{:S(2)}) async-start(), calls=%async_computation.27 | async-start | bytes 1310720 | tf_op jit(solution)/shard_map/all_gather | solution.py:187
  879.4 13.2 copy-start.51
  879.4 425.8 %reduce-scatter.29.cloned.1.call-start = ((), (), s32[]{:S(2)}) async-start(), calls=%async_computation.16 | async-start | bytes 589824 | tf_op jit(solution)/shard_map/reduce_scatter | solution.py:186
  892.6 484.0 %reduce-scatter.37.cloned.1.call-start = ((), (), s32[]{:S(2)}) async-start(), calls=%async_computation.20 | async-start | bytes 2359296 | tf_op jit(solution)/shard_map/reduce_scatter | solution.py:186
  892.6 5.6 copy-start.42
  898.0 49.5 %copy-start.60 = (u32[32]{0:T(128)S(1)}, u32[32]{0:T(128)}, u32[]{:S(2)}) copy-start(u32[32]{0:T(128)} %constant.127) | copy-start | bytes 388
  898.1 546.6 %reduce-scatter.25.cloned.1.call-start = ((), (), s32[]{:S(2)}) async-start(), calls=%async_computation.14 | async-start | bytes 1769472 | tf_op jit(solution)/shard_map/reduce_scatter | solution.py:186
  901.8 561.7 %all-gather.59.cloned.1.call-start = ((), (), s32[]{:S(2)}) async-start(), calls=%async_computation.26 | async-start | bytes 1310720 | tf_op jit(solution)/shard_map/all_gather | solution.py:187
  947.5 534.5 %all-gather.65.cloned.1.call-start = ((), (), s32[]{:S(2)}) async-start(), calls=%async_computation.29 | async-start | bytes 1310720 | tf_op jit(solution)/shard_map/all_gather | solution.py:187
  1082.1 418.3 %all-gather.63.cloned.1.call-start = ((), (), s32[]{:S(2)}) async-start(), calls=%async_computation.28 | async-start | bytes 1310720 | tf_op jit(solution)/shard_map/all_gather | solution.py:187
  1082.1 79.6 %collective-permute-start.3 = (bf16[12,1024]{1,0:T(8,128)(2,1)S(1)}, bf16[12,1024]{1,0:T(8,128)(2,1)S(1)}, u32[]{:S(2)}, u32[]{:S(2)}) collective-permute-start(bf16[12,1024]{1,0:T(8,128)(2,1)S(1)} %slice.249), channel_id=1, source_target_pairs={{0,1},{1,2},{2,3},{4,5},{5,6},{6,7},{8,9},{9,10},{10,11},{12,13},{... | collective-permute-start | bytes 73736
  1160.7 46.4 %copy-start.8 = (f32[148,1024]{1,0:T(8,128)S(1)}, f32[148,1024]{1,0:T(8,128)}, u32[]{:S(2)}) copy-start(f32[148,1024]{1,0:T(8,128)} %copy-done.7) | copy-start | bytes 1818628
  1245.1 131.5 %copy-start.44 = (bf16[128,1,4,256]{0,3,2,1:T(8,128)(2,1)S(1)}, bf16[128,1,4,256]{0,3,2,1:T(8,128)(2,1)}, u32[]{:S(2)}) copy-start(bf16[128,1,4,256]{0,3,2,1:T(8,128)(2,1)} %copy.148) | copy-start | bytes 786436
  (40 other events, 70.9 us)
Sparse Core Ops, SparseCore 0:
  36.4 26.3 all-gather.66
  65.4 43.5 all-gather.42
  111.7 47.8 all-gather.50
  191.0 19.6 all-gather.68
  213.2 49.3 all-gather.44
  265.2 47.6 all-gather.52
  345.8 19.6 all-gather.70
  368.1 43.5 all-gather.46
  413.8 47.7 all-gather.54
  463.0 23.7 all-gather.74
  498.2 19.2 all-gather.72
  519.4 49.3 all-gather.48
  570.9 47.6 all-gather.56
  656.2 19.6 all-gather.76
  726.8 20.1 all-gather.78
  787.4 20.1 all-gather.80
  811.5 65.6 reduce-scatter.34
  880.6 66.7 reduce-scatter.32
  950.8 60.5 reduce-scatter.30
  1015.2 66.7 reduce-scatter.38
  1086.4 64.2 reduce-scatter.26
  1154.0 68.1 all-reduce.20
  1223.9 18.2 all-gather.60
  1245.7 59.4 reduce-scatter.28
  1309.3 67.2 reduce-scatter.36
  1380.4 64.2 reduce-scatter.24
  1446.2 17.3 all-gather.58
  1465.2 16.7 all-gather.64
  1483.6 16.7 all-gather.62

commit v2 on v1

--- a/solution.py
+++ b/solution.py
@@ -4,6 +4,8 @@
 import jax
 import jax.numpy as jnp
 from jax import lax
+from jax.experimental import pallas as pl
+from jax.experimental.pallas import tpu as pltpu
 from jax.sharding import PartitionSpec as P
 
 HEADS = 16
@@ -123,7 +125,7 @@
     return (grad_hidden, (grad_qkv, grad_out, grad_fc1, grad_fc2), rows_sum, grad_bias_proj, grad_bias_fc1)
 
 
-def local(block_input, key_mask, valid, gains, biases, w_qkv, w_out, w_fc1, b_fc1, w_fc2, cotangent):
+def plain_local(block_input, key_mask, valid, gains, biases, w_qkv, w_out, w_fc1, b_fc1, w_fc2, cotangent):
     layers = w_qkv.shape[0]
     groups = lax.axis_size("seq")
     shards = lax.axis_size("dp")
@@ -226,6 +228,728 @@
     )
 
 
+MESH = pl.DeviceIdType.MESH
+NEG = -1000000000.0
+
+
+def ddot(a, b, ca, cb):
+    return lax.dot_general(a, b, (((ca,), (cb,)), ((), ())), preferred_element_type=F32)
+
+
+def fused_kernel(cfg, x_ref, maskrow_ref, tv_ref, small_ref, w_in, cot_ref,
+                 y_ref, gx_ref, tot_ref, o_hbm,
+                 W, WO, XR, ZR, AF, QKV, OB, MF, U, H, H2, LSE,
+                 BF, PB, R0, R1, R2, DU, GW, DQKV, DO, DKV, DH, MK, MR, PS, PR, SGF, SG, SX, SZ, ST, FIN, STAT,
+                 loc_sem, agz_s, agz_r, agx_s, agx_r, ge_s, ge_r, re_s, re_r, wo_s, wo_r, gw_s, gw_r,
+                 rx_s, rx_r, rz_s, rz_r, fo_s, fo_r, mk_s, mk_r, st_s, st_r):
+    L, M, RB, T, TP, D, NC = cfg["L"], cfg["M"], cfg["RB"], cfg["T"], cfg["TP"], cfg["D"], cfg["NC"]
+    S = 4
+    R = S * TP
+    C = D // S
+    FS = cfg["FS"]
+    SCALE = 1.0 / math.sqrt(HEAD_DIM)
+    COLS = (0, 3 * C, 3 * C + C, 3 * C + C + FS, NC)
+    QK, OUT, FC1, FC2 = range(4)
+    d = lax.axis_index("dp")
+    s = lax.axis_index("seq")
+    z = d // 2
+    xx = d % 2
+    ypos = s // 2
+    cpos = s % 2
+    core = (d, s + 1 - 2 * cpos)
+    ydev = (d, s + 2 - 4 * ypos)
+    diag = (d, (s + 1 - 2 * cpos) + 2 - 4 * ypos)
+    xdev = (d + 1 - 2 * xx, s)
+    zof = [lax.rem(z + k, M) for k in range(M)]
+    zdev = [(2 * zof[k] + xx, s) for k in range(M)]
+    zfrom = [lax.rem(z + M - k, M) for k in range(M)]
+
+    def rcopy(src, dst, ss, rs, dev):
+        return pltpu.make_async_remote_copy(src_ref=src, dst_ref=dst, send_sem=ss, recv_sem=rs,
+                                            device_id=dev, device_id_type=MESH)
+
+    bar = pltpu.get_barrier_semaphore()
+    for dev in [core, ydev, diag, xdev] + zdev[1:]:
+        pl.semaphore_signal(bar, inc=1, device_id=dev, device_id_type=MESH)
+    pl.semaphore_wait(bar, 3 + M)
+
+    def wslot(l, zz, xp, j):
+        return W.at[l, zz, xp, :, COLS[j]:COLS[j + 1]]
+
+    def wsrc(l, j):
+        return w_in.at[l, :, COLS[j]:COLS[j + 1]]
+
+    def ag_pair(p, zz, xp):
+        if p == 0:
+            return PS.at[zz, xp]
+        l, j = divmod(p - 1, 4)
+        return wslot(l, zz, xp, j)
+
+    def ag_own(p):
+        if p == 0:
+            return small_ref
+        l, j = divmod(p - 1, 4)
+        return wsrc(l, j)
+
+    def ag_z(p, k):
+        return rcopy(ag_own(p), ag_pair(p, z, xx), agz_s.at[p, k], agz_r.at[p, z], zdev[k])
+
+    def ag_z_recv(p, k):
+        zz = zfrom[k]
+        return rcopy(ag_own(p), ag_pair(p, zz, xx), agz_s.at[p, k], agz_r.at[p, zz], zdev[k])
+
+    def ag_x(p, zz, own):
+        src = ag_own(p) if own else ag_pair(p, zz, xx)
+        return rcopy(src, ag_pair(p, zz, xx), agx_s.at[p, zz], agx_r.at[p, zz], xdev)
+
+    def ag_x_recv(p, zz):
+        return rcopy(ag_own(p), ag_pair(p, zz, 1 - xx), agx_s.at[p, zz], agx_r.at[p, zz], xdev)
+
+    def ag_issue(p):
+        for k in range(1, M):
+            ag_z(p, k).start()
+        ag_x(p, z, True).start()
+
+    NP = 1 + 4 * L
+    queue = [(p, k) for p in range(NP) for k in range(1, M)]
+    state = {"next": 0, "issued": 0}
+
+    def ag_issue_to(n):
+        while state["issued"] < min(n, NP):
+            ag_issue(state["issued"])
+            state["issued"] += 1
+
+    def ag_service(n):
+        for _ in range(n):
+            if state["next"] == len(queue):
+                return
+            p, k = queue[state["next"]]
+            ag_issue_to(p + 1)
+            ag_z_recv(p, k).wait_recv()
+            ag_x(p, zfrom[k], False).start()
+            state["next"] += 1
+            if k == M - 1:
+                ag_issue_to(p + 1 + cfg["ahead"])
+
+    def ag_finish(p):
+        while state["next"] < (p + 1) * (M - 1):
+            ag_service(1)
+        for k in range(M):
+            ag_x_recv(p, zfrom[k]).wait_recv()
+
+    def ag_drain():
+        for p in range(NP):
+            for k in range(1, M):
+                ag_z(p, k).wait_send()
+            for k in range(M):
+                ag_x(p, zof[k], k == 0).wait_send()
+
+    locs = []
+    for l in range(L):
+        locs.append(pltpu.make_async_copy(w_in.at[l], W.at[l, z, xx], loc_sem.at[l]))
+    ag_issue_to(1 + cfg["ahead"])
+    for c in locs:
+        c.start()
+    PS[z, xx] = small_ref[...]
+    MK[s] = maskrow_ref[...]
+    mks = [rcopy(maskrow_ref, MK.at[s], mk_s.at[i], mk_r.at[i], dev) for i, dev in enumerate((core, ydev, diag))]
+    for c in mks:
+        c.start()
+    H[0] = jnp.zeros((TP, D), F32)
+    H[0, 0:T, :] = x_ref[...].astype(F32)
+    SGF[...] = jnp.zeros_like(SGF)
+    SG[...] = jnp.zeros_like(SG)
+    STAT[...] = jnp.zeros_like(STAT)
+    for c in mks:
+        c.wait()
+    MR[...] = (MK[0] + MK[1]) + (MK[2] + MK[3])
+    ag_finish(0)
+    for i in range(M):
+        for j in range(2):
+            PR[:, 128 * (2 * i + j):128 * (2 * i + j) + 128] = PS[i, j]
+    for c in locs:
+        c.wait()
+
+    def prow(l, i):
+        return PR[12 * l + i:12 * l + i + 1, :]
+
+    def prow_cols(l, i):
+        return PR[12 * l + i:12 * l + i + 1, pl.ds(pl.multiple_of(C * s, C), C)]
+
+    HB = TP // 2
+
+    def ge_part(e, buf, i, h):
+        rows = pl.ds(h * HB, HB)
+        if i == 0:
+            return rcopy(buf.at[s, rows], buf.at[s, rows], ge_s.at[e, 0, h], ge_r.at[e, 0, h], core)
+        if i == 1:
+            return rcopy(buf.at[s, rows], buf.at[s, rows], ge_s.at[e, 1, h], ge_r.at[e, 1, h], ydev)
+        return rcopy(buf.at[ydev[1], rows], buf.at[ydev[1], rows], ge_s.at[e, 2, h], ge_r.at[e, 2, h], core)
+
+    def ge_start(e, buf):
+        for h in range(2):
+            ge_part(e, buf, 1, h).start()
+        for h in range(2):
+            ge_part(e, buf, 0, h).start()
+
+    def ge_end(e, buf):
+        for h in range(2):
+            rcopy(buf.at[s, pl.ds(h * HB, HB)], buf.at[ydev[1], pl.ds(h * HB, HB)],
+                  ge_s.at[e, 1, h], ge_r.at[e, 1, h], ydev).wait_recv()
+            ge_part(e, buf, 2, h).start()
+        for h in range(2):
+            rcopy(buf.at[s, pl.ds(h * HB, HB)], buf.at[core[1], pl.ds(h * HB, HB)],
+                  ge_s.at[e, 0, h], ge_r.at[e, 0, h], core).wait_recv()
+        for h in range(2):
+            rcopy(buf.at[ydev[1], pl.ds(h * HB, HB)], buf.at[diag[1], pl.ds(h * HB, HB)],
+                  ge_s.at[e, 2, h], ge_r.at[e, 2, h], core).wait_recv()
+        for i in range(3):
+            for h in range(2):
+                ge_part(e, buf, i, h).wait_send()
+
+    def re_copy(e, i):
+        b = e % 2
+        if i == 0:
+            return rcopy(PB.at[b, 1 - ypos, 1 - cpos], R0.at[b], re_s.at[e, 0], re_r.at[e, 0], core)
+        if i == 1:
+            return rcopy(PB.at[b, 1 - ypos, cpos], R1.at[b], re_s.at[e, 1], re_r.at[e, 1], ydev)
+        return rcopy(PB.at[b, ypos, 1 - cpos], R2.at[b], re_s.at[e, 2], re_r.at[e, 2], core)
+
+    def re_run(e, partial):
+        b = e % 2
+        partial(1 - ypos, b)
+        re_copy(e, 0).start()
+        re_copy(e, 0).wait_recv()
+
+        def add(i, _):
+            rows = pl.ds(pl.multiple_of(i * 16, 16), 16)
+            PB[b, 1 - ypos, cpos, rows, :] = (PB[b, 1 - ypos, cpos, rows, :].astype(F32) + R0[b, rows, :].astype(F32)).astype(BF16)
+            return 0
+        lax.fori_loop(0, TP // 16, add, 0)
+        re_copy(e, 1).start()
+        partial(ypos, b)
+        re_copy(e, 2).start()
+
+    def re_end(e):
+        for i in (2, 1):
+            re_copy(e, i).wait_recv()
+        for i in range(3):
+            re_copy(e, i).wait_send()
+
+    def re_rows(e, rows):
+        b = e % 2
+        return (PB[b, ypos, cpos, rows, :].astype(F32) + R2[b, rows, :].astype(F32)) + R1[b, rows, :].astype(F32)
+
+    def partial_of(lhs, rhs, cb):
+        def run(chip, b):
+            def tile(j, _):
+                cols = pl.ds(pl.multiple_of(j * C, C), C)
+                r = ddot(lhs(chip), rhs(j), 1, cb).astype(BF16)
+                PB[b, chip, :, :, cols] = r.reshape(2, TP, C)
+                return 0
+            lax.fori_loop(0, S, tile, 0)
+        return run
+
+    def row_loop(body, init):
+        def one(i, carry):
+            return body(pl.ds(pl.multiple_of(i * 16, 16), 16), carry)
+        return lax.fori_loop(0, TP // 16, one, init)
+
+    def norm(v):
+        center = v - jnp.mean(v, -1, keepdims=True)
+        inverse = lax.rsqrt(jnp.mean(center * center, -1, keepdims=True) + epsilon)
+        return center * inverse, inverse
+
+    def fold(v):
+        return v[0:8] + v[8:16]
+
+    def col_sum(v):
+        return jnp.sum(v, axis=0, keepdims=True)
+
+    lane_low = lax.broadcasted_iota(jnp.int32, (1, 2 * HEAD_DIM), 1) < HEAD_DIM
+    lane_idx = lax.broadcasted_iota(jnp.int32, (1, 128), 1)
+
+    def attend(l, pair):
+        def block(i, _):
+            rows = pl.ds(pl.multiple_of(i * TP, 16), TP)
+            q = QKV[l, rows, 128 * pair:128 * pair + 128]
+            k = QKV[l, :, C + 128 * pair:C + 128 * pair + 128]
+            v = QKV[l, :, 2 * C + 128 * pair:2 * C + 128 * pair + 128]
+            outs, lses = [], []
+            for h in range(2):
+                keep = lane_low if h == 0 else jnp.logical_not(lane_low)
+                qh = jnp.where(keep, q, jnp.zeros_like(q))
+                sc = ddot(qh, k, 1, 1) * SCALE
+                sc = jnp.where(MR[0:1, :] > 0, sc, NEG)
+                mx = jnp.max(sc, -1, keepdims=True)
+                ex = jnp.exp(sc - mx)
+                tot = jnp.sum(ex, -1, keepdims=True)
+                outs.append(ddot(ex.astype(BF16), v, 1, 0) / tot)
+                lses.append(mx + jnp.log(tot))
+            OB[l, rows, 128 * pair:128 * pair + 128] = jnp.where(lane_low, outs[0], outs[1]).astype(BF16)
+            LSE[l, pair, rows, :] = jnp.where(lane_idx == 0, lses[0], lses[1])
+            return 0
+        lax.fori_loop(0, S, block, 0)
+
+    def attend_back(l, pair):
+        DKV[...] = jnp.zeros_like(DKV)
+
+        def block(i, _):
+            rows = pl.ds(pl.multiple_of(i * TP, 16), TP)
+            q = QKV[l, rows, 128 * pair:128 * pair + 128]
+            k = QKV[l, :, C + 128 * pair:C + 128 * pair + 128]
+            v = QKV[l, :, 2 * C + 128 * pair:2 * C + 128 * pair + 128]
+            do = DO[rows, 128 * pair:128 * pair + 128]
+            lse = LSE[l, pair, rows, :]
+            dqs = []
+            dk = dv = None
+            for h in range(2):
+                keep = lane_low if h == 0 else jnp.logical_not(lane_low)
+                qh = jnp.where(keep, q, jnp.zeros_like(q))
+                doh = jnp.where(keep, do, jnp.zeros_like(do))
+                sc = ddot(qh, k, 1, 1) * SCALE
+                sc = jnp.where(MR[0:1, :] > 0, sc, NEG)
+                p = jnp.exp(sc - lse[:, h:h + 1])
+                dp = ddot(doh, v, 1, 1)
+                inner = jnp.sum(p * dp, -1, keepdims=True)
+                ds = (p * (dp - inner)).astype(BF16)
+                dqs.append(ddot(ds, k, 1, 0))
+                dkh = ddot(ds, qh, 0, 0)
+                dvh = ddot(p.astype(BF16), doh, 0, 0)
+                dk = dkh if dk is None else dk + dkh
+                dv = dvh if dv is None else dv + dvh
+            DQKV[rows, 128 * pair:128 * pair + 128] = (jnp.where(lane_low, dqs[0], dqs[1]) * SCALE).astype(BF16)
+            DKV[0] += dk
+            DKV[1] += dv
+            return 0
+        lax.fori_loop(0, S, block, 0)
+        DQKV[:, C + 128 * pair:C + 128 * pair + 128] = (DKV[0] * SCALE).astype(BF16)
+        DQKV[:, 2 * C + 128 * pair:2 * C + 128 * pair + 128] = DKV[1].astype(BF16)
+
+    peers = (core, ydev, diag)
+
+    def wo_copy(l, i):
+        to = peers[i][1]
+        return rcopy(W.at[l, to, :, :, COLS[OUT]:COLS[FC1]], WO.at[l, :, :, pl.ds(pl.multiple_of(C * s, C), C)],
+                     wo_s.at[l, i], wo_r.at[l, i], peers[i])
+
+    def wo_start(l):
+        for i in range(3):
+            wo_copy(l, i).start()
+        WO[l, :, :, pl.ds(pl.multiple_of(C * s, C), C)] = W[l, s, :, :, COLS[OUT]:COLS[FC1]]
+
+    def wo_end(l):
+        for i in range(3):
+            wo_copy(l, i).wait()
+
+    def gw_copy(l, i):
+        to = peers[i][1]
+        return rcopy(WO.at[l, :, :, pl.ds(pl.multiple_of(C * to, C), C)], W.at[l, s, :, :, COLS[OUT]:COLS[FC1]],
+                     gw_s.at[l, i], gw_r.at[l, i], peers[i])
+
+    def gw_start(l):
+        for i in range(3):
+            gw_copy(l, i).start()
+        W[l, s, :, :, COLS[OUT]:COLS[FC1]] = WO[l, :, :, pl.ds(pl.multiple_of(C * s, C), C)]
+
+    def gw_end(l):
+        for i in range(3):
+            gw_copy(l, i).wait()
+
+    def wtile(l, j, a, b):
+        n = M // S
+        if n == 1:
+            return W[l, j, :, :, a:b].reshape(2 * RB, b - a)
+        return W[l, pl.ds(j * n, n), :, :, a:b].reshape(2 * RB * n, b - a)
+
+    def forward(l):
+        e = 2 * l
+
+        def ln1(rows, _):
+            n, _r = norm(H[l, rows, :])
+            AF[l, s, rows, :] = (n * prow(l, 0) + prow(l, 2)).astype(BF16)
+            return 0
+        row_loop(ln1, 0)
+        ge_start(e, AF.at[l])
+        ag_service(3)
+        ge_end(e, AF.at[l])
+        ag_finish(1 + 4 * l + QK)
+        for n in range(3):
+            r = ddot(AF[l].reshape(R, D), W[l, :, :, :, C * n:C * n + C].reshape(D, C), 1, 0)
+            if n == 0:
+                r = r + prow_cols(l, 3)
+            if n == 2:
+                r = r + prow_cols(l, 4)
+            QKV[l, :, C * n:C * n + C] = r.astype(BF16)
+        ag_finish(1 + 4 * l + OUT)
+        wo_start(l)
+        attend(l, 0)
+        ag_service(1)
+        attend(l, 1)
+        ag_service(1)
+        wo_end(l)
+        re_run(e + 0, partial_of(
+            lambda chip: OB[l, pl.ds(pl.multiple_of(chip * 2 * TP, 16), 2 * TP), :],
+            lambda j: WO[l, :, :, pl.ds(pl.multiple_of(j * C, C), C)].reshape(C, C), 0))
+        ag_service(1)
+        re_end(e + 0)
+
+        def post(rows, acc):
+            hv = H[l, rows, :]
+            br = re_rows(e + 0, rows) + prow(l, 5)
+            mid = hv + br
+            H2[l, rows, :] = mid
+            n, _r = norm(mid)
+            MF[l, s, rows, :] = (n * prow(l, 1) + prow(l, 6)).astype(BF16)
+            t = tv_ref[rows, 0:1]
+            return acc[0] + fold(t * hv * hv), acc[1] + fold(t * br * br)
+        zero = jnp.zeros((8, D), F32)
+        s0, s1 = row_loop(post, (zero, zero))
+        ge_start(e + 1, MF.at[l])
+        ag_service(2)
+        ge_end(e + 1, MF.at[l])
+        ag_finish(1 + 4 * l + FC1)
+        bias = PR[pl.ds(12 * l + 8 + s, 1), :]
+        for j in range(FS // C):
+            u = ddot(MF[l].reshape(R, D), W[l, :, :, :, COLS[FC1] + C * j:COLS[FC1] + C * j + C].reshape(D, C), 1, 0)
+            u = u + bias[:, C * j:C * j + C]
+            U[l, :, C * j:C * j + C] = u
+            GW[:, C * j:C * j + C] = (u / (1.0 + jnp.exp(-1.702 * u))).astype(BF16)
+        ag_finish(1 + 4 * l + FC2)
+        re_run(e + 1, partial_of(
+            lambda chip: GW[pl.ds(pl.multiple_of(chip * 2 * TP, 16), 2 * TP), :],
+            lambda j: W[l, :, :, :, pl.ds(pl.multiple_of(COLS[FC2] + j * C, C), C)].reshape(FS, C), 0))
+        ag_service(2)
+        re_end(e + 1)
+
+        def last(rows, acc):
+            out = re_rows(e + 1, rows) + prow(l, 7)
+            res = H2[l, rows, :] + out
+            H[l + 1, rows, :] = res
+            t = tv_ref[rows, 0:1]
+            return acc + fold(t * out * out)
+        s2 = row_loop(last, zero)
+        for i, v in enumerate((s0, s1, s2)):
+            STAT[...] = jnp.where(lane_idx == 3 * l + i, jnp.sum(col_sum(v), axis=1, keepdims=True), STAT[...])
+
+    for l in range(L):
+        forward(l)
+    STAT[...] = jnp.where(lane_idx == 3 * L, col_sum(tv_ref[:, 0:1]), STAT[...])
+    y_ref[...] = H[L, 0:T, :].astype(BF16)
+    ag_drain()
+
+    def rx_copy(l, j):
+        a, b = COLS[j], COLS[j + 1]
+        return rcopy(W.at[l, :, 1 - xx, :, a:b], XR.at[l, :, :, a:b], rx_s.at[l, j], rx_r.at[l, j], xdev)
+
+    def rz_copy(l, j, k):
+        a, b = COLS[j], COLS[j + 1]
+        return rcopy(XR.at[l, zof[k], :, a:b], ZR.at[l, z, :, a:b], rz_s.at[l, j, k], rz_r.at[l, j, k], zdev[k])
+
+    def rz_recv(l, j, k):
+        a, b = COLS[j], COLS[j + 1]
+        return rcopy(XR.at[l, zof[k], :, a:b], ZR.at[l, zfrom[k], :, a:b], rz_s.at[l, j, k], rz_r.at[l, j, k], zdev[k])
+
+    def fo_copy(l, j, i):
+        a, b = COLS[j], COLS[j + 1]
+        return rcopy(FIN.at[l, :, a:b], o_hbm.at[l, s, :, a:b], fo_s.at[l, j, i], fo_r.at[l, j, i], peers[i])
+
+    def fo_recv(l, j, i):
+        a, b = COLS[j], COLS[j + 1]
+        return rcopy(FIN.at[l, :, a:b], o_hbm.at[l, peers[i][1], :, a:b], fo_s.at[l, j, i], fo_r.at[l, j, i], peers[i])
+
+    def fo_local(l, j):
+        a, b = COLS[j], COLS[j + 1]
+        return pltpu.make_async_copy(FIN.at[l, :, a:b], o_hbm.at[l, s, :, a:b], loc_sem.at[L + 4 * l + j])
+
+    def red_first(l, j):
+        a, b = COLS[j], COLS[j + 1]
+        rx_copy(l, j).wait_recv()
+        for k in list(range(1, M)) + [0]:
+            zz = zof[k]
+            for r0 in range(0, RB, 32):
+                XR[l, zz, r0:r0 + 32, a:b] = (XR[l, zz, r0:r0 + 32, a:b].astype(F32) + W[l, zz, xx, r0:r0 + 32, a:b].astype(F32)).astype(BF16)
+            if k > 0:
+                rz_copy(l, j, k).start()
+
+    def red_second(l, j):
+        a, b = COLS[j], COLS[j + 1]
+        for k in range(1, M):
+            rz_recv(l, j, k).wait_recv()
+        for r0 in range(0, RB, 32):
+            t = XR[l, z, r0:r0 + 32, a:b].astype(F32)
+            for k in range(1, M):
+                t = t + ZR[l, zfrom[k], r0:r0 + 32, a:b].astype(F32)
+            FIN[l, r0:r0 + 32, a:b] = t.astype(BF16)
+        for i in range(3):
+            fo_copy(l, j, i).start()
+        fo_local(l, j).start()
+
+    def red_end(l, j):
+        rx_copy(l, j).wait_send()
+        for k in range(1, M):
+            rz_copy(l, j, k).wait_send()
+        for i in range(3):
+            fo_copy(l, j, i).wait_send()
+            fo_recv(l, j, i).wait_recv()
+        fo_local(l, j).wait()
+
+    events = []
+    done = {"n": 0}
+
+    def red_push(l, j):
+        rx_copy(l, j).start()
+        events.append((red_first, l, j))
+
+    def red_service(n):
+        for _ in range(n):
+            if done["n"] >= len(events):
+                return
+            f, l, j = events[done["n"]]
+            done["n"] += 1
+            f(l, j)
+            if f is red_first:
+                events.insert(min(done["n"] + 1, len(events)), (red_second, l, j))
+
+    def norm_back(l, src, e, gain):
+        def one(rows, acc):
+            n, r = norm(src[l, rows, :])
+            dm = re_rows(e, rows)
+            dn = dm * gain
+            pm = jnp.mean(dn, -1, keepdims=True)
+            cm = jnp.mean(dn * n, -1, keepdims=True)
+            DH[rows, :] = DH[rows, :] + r * (dn - pm - n * cm)
+            return acc[0] + fold(dm * n), acc[1] + fold(dm)
+        zero = jnp.zeros((8, D), F32)
+        g, b = row_loop(one, (zero, zero))
+        return col_sum(g), col_sum(b)
+
+    def low_of(buf):
+        def one(rows, acc):
+            v = DH[rows, :].astype(BF16)
+            buf[s, rows, :] = v
+            return acc + fold(v.astype(F32))
+        return col_sum(row_loop(one, jnp.zeros((8, D), F32)))
+
+    def backward(l):
+        ge_a = re_a = 2 * L + 2 * (L - 1 - l)
+        ge_b = re_b = ge_a + 1
+        B0, B1 = BF.at[0], BF.at[1]
+        SGF[12 * l + 7:12 * l + 8, :] = low_of(B0)
+        ge_start(ge_a, B0)
+        red_service(1)
+        ge_end(ge_a, B0)
+        for j in range(FS // C):
+            dg = ddot(BF[0].reshape(R, D), wtile(l, j, COLS[FC2], COLS[FC2] + D), 1, 1)
+            u = U[l, :, C * j:C * j + C]
+            sg = 1.0 / (1.0 + jnp.exp(-1.702 * u))
+            GW[:, C * j:C * j + C] = (u * sg).astype(BF16)
+            du = (dg * (sg + 1.702 * u * sg * (1.0 - sg))).astype(BF16)
+            DU[:, C * j:C * j + C] = du
+            SGF[pl.ds(12 * l + 8 + s, 1), C * j:C * j + C] = jnp.sum(du.astype(F32), axis=0, keepdims=True)
+        red_service(1)
+        for j in range(FS // C):
+            W[l, j, :, :, COLS[FC2]:COLS[FC2] + D] = ddot(GW[:, C * j:C * j + C], BF[0].reshape(R, D), 0, 0).astype(BF16).reshape(2, RB, D)
+        red_push(l, FC2)
+        re_run(re_a, partial_of(
+            lambda chip: DU[pl.ds(pl.multiple_of(chip * 2 * TP, 16), 2 * TP), :],
+            lambda j: wtile(l, j, COLS[FC1], COLS[FC1] + FS), 1))
+        for j in range(S):
+            W[l, j, :, :, COLS[FC1]:COLS[FC1] + FS] = ddot(MF[l, :, :, C * j:C * j + C].reshape(R, C), DU[...], 0, 0).astype(BF16).reshape(2, RB, FS)
+        red_push(l, FC1)
+        re_end(re_a)
+        gg, bb = norm_back(l, H2, re_a, prow(l, 1))
+        SGF[12 * l + 1:12 * l + 2, :] = gg
+        SGF[12 * l + 6:12 * l + 7, :] = bb
+        SGF[12 * l + 5:12 * l + 6, :] = low_of(B1)
+        ge_start(ge_b, B1)
+        red_service(1)
+        ge_end(ge_b, B1)
+        DO[...] = ddot(BF[1].reshape(R, D), WO[l].reshape(C, D), 1, 1).astype(BF16)
+        for j in range(S):
+            WO[l, :, :, C * j:C * j + C] = ddot(OB[l], BF[1, :, :, C * j:C * j + C].reshape(R, C), 0, 0).astype(BF16).reshape(2, RB, C)
+        gw_start(l)
+        attend_back(l, 0)
+        red_service(1)
+        attend_back(l, 1)
+        gw_end(l)
+        red_push(l, OUT)
+        red_service(1)
+        for i, (row, c0) in enumerate(((3, 0), (4, 2 * C))):
+            SGF[12 * l + row:12 * l + row + 1, pl.ds(pl.multiple_of(C * s, C), C)] = jnp.sum(
+                DQKV[:, c0:c0 + C].astype(F32), axis=0, keepdims=True)
+        re_run(re_b, partial_of(
+            lambda chip: DQKV[pl.ds(pl.multiple_of(chip * 2 * TP, 16), 2 * TP), :],
+            lambda j: wtile(l, j, 0, 3 * C), 1))
+        for j in range(S):
+            W[l, j, :, :, 0:3 * C] = ddot(AF[l, :, :, C * j:C * j + C].reshape(R, C), DQKV[...], 0, 0).astype(BF16).reshape(2, RB, 3 * C)
+        red_push(l, QK)
+        re_end(re_b)
+        gg, bb = norm_back(l, H, re_b, prow(l, 0))
+        SGF[12 * l + 0:12 * l + 1, :] = gg
+        SGF[12 * l + 2:12 * l + 3, :] = bb
+
+    DH[...] = jnp.zeros_like(DH)
+    DH[0:T, :] = cot_ref[...].astype(F32) * tv_ref[0:T, 0:1]
+    for l in reversed(range(L)):
+        backward(l)
+    gx_ref[...] = DH[0:T, :]
+
+    for i in range(M):
+        for j in range(2):
+            SG[i, j, 0:24, :] = SGF[0:24, 128 * (2 * i + j):128 * (2 * i + j) + 128]
+            SG[i, j, 24:25, :] = STAT[...]
+    sgx = rcopy(SG.at[:, 1 - xx], SX, st_s.at[0], st_r.at[0], xdev)
+    sgx.start()
+    sgx.wait()
+    SX[...] = SX[...] + SG[:, xx]
+    SZ[z] = SX[z]
+
+    def sz(k, frm):
+        return rcopy(SX.at[zof[k]], SZ.at[zfrom[k] if frm else z], st_s.at[k], st_r.at[k], zdev[k])
+    for k in range(1, M):
+        sz(k, False).start()
+    red_service(2)
+    for k in range(1, M):
+        sz(k, True).wait_recv()
+    tot = SZ[0]
+    for k in range(1, M):
+        tot = tot + SZ[k]
+    ST[s] = tot
+
+    def stc(i, frm):
+        slot = peers[i][1] if frm else s
+        return rcopy(ST.at[s], ST.at[slot], st_s.at[M + i], st_r.at[M + i], peers[i])
+    for i in range(3):
+        stc(i, False).start()
+    while done["n"] < len(events):
+        red_service(1)
+    for i in range(3):
+        stc(i, True).wait_recv()
+    tot_ref[...] = (ST[0] + ST[1]) + (ST[2] + ST[3])
+    for k in range(1, M):
+        sz(k, False).wait_send()
+    for i in range(3):
+        stc(i, False).wait_send()
+    for l in reversed(range(L)):
+        for j in (FC2, FC1, OUT, QK):
+            red_end(l, j)
+
+
+def fused_local(cfg, block_input, key_mask, valid, gains, biases, w_qkv, w_out, w_fc1, b_fc1, w_fc2, cotangent):
+    L, M, RB, T, TP, D, NC, FS = (cfg[n] for n in ("L", "M", "RB", "T", "TP", "D", "NC", "FS"))
+    S, dp = 4, 2 * M
+    me = lax.axis_index("seq")
+    C = D // S
+    R = S * TP
+
+    def columns(w, outer):
+        view = w.reshape(L, RB, outer, S, -1)
+        return lax.dynamic_index_in_dim(view, me, 3, False).reshape(L, RB, -1)
+
+    w_in = jnp.concatenate([
+        columns(w_qkv, 3), columns(w_out, 1), columns(w_fc1, dp),
+        lax.dynamic_index_in_dim(w_fc2.reshape(L, S, RB, D), me, 1, False)], 2)
+    small = jnp.concatenate([gains, biases, b_fc1.reshape(L, S, -1)], 1).astype(F32).reshape(L * 12, RB)
+    mask = jnp.pad(key_mask[0].astype(F32), (0, TP - T))
+    mask_row = jnp.where(jnp.arange(S)[:, None] == me, mask[None, :], 0.0).reshape(1, R)
+    mask_row = jnp.broadcast_to(mask_row, (8, R))
+    tv = jnp.broadcast_to((mask * valid[0].astype(F32))[:, None], (TP, 128))
+    vm = pl.BlockSpec(memory_space=pltpu.VMEM)
+    hbm = pl.BlockSpec(memory_space=pl.ANY)
+    dma = pltpu.SemaphoreType.DMA
+    v = pltpu.VMEM
+    NP, NE = 1 + 4 * L, 4 * L
+    y, gx, tot, og = pl.pallas_call(
+        partial(fused_kernel, cfg),
+        out_shape=(
+            jax.ShapeDtypeStruct((T, D), BF16),
+            jax.ShapeDtypeStruct((T, D), F32),
+            jax.ShapeDtypeStruct((32, RB), F32),
+            jax.ShapeDtypeStruct((L, S, RB, NC), BF16),
+        ),
+        in_specs=[vm, vm, vm, vm, hbm, vm],
+        out_specs=(vm, vm, vm, hbm),
+        scratch_shapes=[
+            v((L, M, 2, RB, NC), BF16),
+            v((L, 2, RB, D), BF16),
+            v((L, M, RB, NC), BF16),
+            v((L, M, RB, NC), BF16),
+            v((L, S, TP, D), BF16),
+            v((L, R, 3 * C), BF16),
+            v((L, R, C), BF16),
+            v((L, S, TP, D), BF16),
+            v((L, R, FS), F32),
+            v((L + 1, TP, D), F32),
+            v((L, TP, D), F32),
+            v((L, 2, R, 128), F32),
+            v((2, S, TP, D), BF16),
+            v((2, 2, 2, TP, D), BF16),
+            v((2, TP, D), BF16),
+            v((2, TP, D), BF16),
+            v((2, TP, D), BF16),
+            v((R, FS), BF16),
+            v((R, FS), BF16),
+            v((R, 3 * C), BF16),
+            v((R, C), BF16),
+            v((2, R, 128), F32),
+            v((TP, D), F32),
+            v((S, 8, R), F32),
+            v((8, R), F32),
+            v((M, 2, 12 * L, RB), F32),
+            v((12 * L, D), F32),
+            v((12 * L, D), F32),
+            v((M, 2, 32, RB), F32),
+            v((M, 32, RB), F32),
+            v((M, 32, RB), F32),
+            v((S, 32, RB), F32),
+            v((L, RB, NC), BF16),
+            v((1, RB), F32),
+            dma((5 * L,)),
+            dma((NP, M)), dma((NP, M)), dma((NP, M)), dma((NP, M)),
+            dma((NE, 3, 2)), dma((NE, 3, 2)), dma((NE, 3)), dma((NE, 3)),
+            dma((L, 3)), dma((L, 3)), dma((L, 3)), dma((L, 3)),
+            dma((L, 4)), dma((L, 4)), dma((L, 4, M)), dma((L, 4, M)),
+            dma((L, 4, 3)), dma((L, 4, 3)), dma((3,)), dma((3,)), dma((M + 3,)), dma((M + 3,)),
+        ],
+        compiler_params=pltpu.CompilerParams(
+            collective_id=0, has_side_effects=True, vmem_limit_bytes=cfg["vmem"]),
+        cost_estimate=pl.CostEstimate(flops=24_000_000_000, bytes_accessed=20_000_000, transcendentals=0),
+    )(block_input[0], mask_row, tv, small, w_in, cotangent[0])
+    g = og.astype(F32)
+    parts = (g[..., :3 * C], g[..., 3 * C:4 * C], g[..., 4 * C:4 * C + FS], g[..., 4 * C + FS:])
+    join = lambda a, outer: a.reshape(L, S, RB, outer, -1).transpose(0, 2, 3, 1, 4).reshape(L, RB, -1)
+    rows = tot[:12 * L].reshape(L, 12, RB)
+    rms = jnp.sqrt(tot[24, :3 * L].reshape(L, 3) / (jnp.maximum(tot[24, 3 * L], 1.0) * D))
+    return (
+        y[None],
+        gx[None],
+        rms,
+        rows[:, :2],
+        jnp.concatenate([rows[:, 2:3], rows[:, 4:8]], 1),
+        rows[:, 3],
+        join(parts[0], 3),
+        join(parts[1], 1),
+        join(parts[2], dp),
+        rows[:, 8:12].reshape(L, S * RB),
+        parts[3].reshape(L, S * RB, D),
+    )
+
+
+def local(*args):
+    block_input, w_qkv, w_fc2 = args[0], args[5], args[9]
+    L, RB = w_qkv.shape[:2]
+    T, D = block_input.shape[1:]
+    S, dp = lax.axis_size("seq"), lax.axis_size("dp")
+    FS = w_fc2.shape[1] * dp // S
+    fits = (S == 4 and dp == 2 * S and RB % 128 == 0 and D // S == 2 * RB and L * 12 + 1 <= 32
+            and FS // dp == RB and HEAD_DIM * 2 == 128 and D // S == 4 * HEAD_DIM and block_input.shape[0] == 1)
+    if not fits:
+        return plain_local(*args)
+    cfg = dict(L=L, M=dp // 2, RB=RB, T=T, TP=-(-T // 16) * 16, D=D, NC=D + 2 * FS, FS=FS, ahead=2, vmem=60 * 2**20)
+    return fused_local(cfg, *args)
+
+
 def solution(mesh):
     return jax.shard_map(
         local,

time: 1520 us -> 522 us (0.34)
  waiting for transfers between devices: 932 us -> 0 us
  Pallas kernels: 0 us -> 448 us
  blocking collectives: 267 us -> 0 us
  matrix products: 110 us -> 0 us
  local copies, waits for them, and re-layouts: 114 us -> 53.9 us
  other arithmetic: 56.8 us -> 7.88 us
  between operations: 18.6 us -> 2.68 us
    all_gather x20 -> x0, waiting for transfers between devices: 473 us -> none  [the longest x8 349 us: gather(): return lax.all_gather(w, 'dp', axis=0, tiled=True)]
    pallas_call x0 -> x1, Pallas kernels: none -> 448 us  [fused_local(): pl.pallas_call(partial(fused_kernel, cfg), out_shape=(jax.ShapeDtypeStruc...]
    reduce_scatter x8 -> x0, waiting for transfers between devices: 425 us -> none  [reduce_(): g = lax.psum_scatter(g, 'dp', scatter_dimension=0, tiled=True)]
    unnamed x8 -> x0, blocking collectives: 135 us -> none
    dot_general x36 -> x0, matrix products: 110 us -> none  [the longest x24 84.4 us: dot(): lax.dot_general(a, b, (((ca,), (cb,)), ((), ())), preferred_element_type=...]
    unnamed x183 -> x17, local copies, waits for them, and re-layouts: 72.8 us -> 13.2 us
    all_gather x5 -> x0, blocking collectives: 58.6 us -> none  [the longest x4 36.1 us: reduce_(): return lax.all_gather(g, 'seq', axis=0)]
    psum x2 -> x0, blocking collectives: 49.2 us -> none  [the longest x1 38.6 us: local(): lax.psum(jnp.concatenate([jnp.stack(stats).reshape(-1), jnp.sum(tok_valid...]
  transfers between devices with their start and end apart: 37 -> 0, of which waited for: 33 -> 0; matrix products, arithmetic and copies ran while one was open for 14% -> 0% of each run, Pallas kernels for 0% -> 0%
where the time goes in v2:
time: 522 us; the launch traced here: 513 us
  Pallas kernels  448 us (86%)
  local copies, waits for them, and re-layouts  53.9 us (10%)
  other arithmetic  7.88 us (2%)
    pallas_call x1, Pallas kernels, fused_local(): pl.pallas_call(partial(fused_kernel, cfg), out_shape=(jax.ShapeDtypeStruc...  448 us
    unnamed x17, local copies, waits for them, and re-layouts  13.2 us

profile of v2, /device:TPU:23, one launch (start us, length us, event | category | flops | bytes accessed | tf_op | source)
XLA Modules:
  0.0 512.9 jit_solution(5190531319547160778)
XLA Ops:
  0.6 0.0 copy-start
  1.5 0.7 convert_element_type.24
  2.2 0.1 broadcast_select_fusion
  2.2 0.1 select_n.22
  2.3 0.6 broadcast_in_dim.42.maskrow_ref
  2.9 0.7 broadcast_in_dim.43.tv_ref
  3.6 0.7 copy.48
  4.3 0.7 maximum_convert_fusion
  5.1 0.6 reshape.129.small_ref
  5.7 0.0 copy-done
  5.7 3.2 reshape.117
  8.9 3.1 dynamic-slice_reduce_fusion
  12.0 0.2 reshape.118
  12.2 1.4 reshape.115
  13.7 0.3 constant_dynamic-slice_fusion
  14.0 1.9 copy.51
  16.0 0.2 copy.55
  16.1 1.3 pad_maximum_fusion.w_in
  17.4 448.4 %shard_map.194 = (bf16[148,1024]{1,0:T(8,128)(2,1)}, f32[148,1024]{1,0:T(8,128)}, f32[32,128]{1,0:T(8,128)}, bf16[2,4,128,3072]{3,2,1,0:T(8,128)(2,1)}) custom-call(bf16[148,1024]{1,0:T(8,128)(2,1)} %bitcast.59, f32[8,640]{1,0:T(8,128)} %broadcast_in_dim.42.maskrow_ref, f32[160,128]{1,0:T(8,128)} %broadcast_in_dim.43.tv_ref, f32[24,128]{1,0:T(8,128)} %reshape.129.small_ref, ...), custom_call_target="tpu_custom_call" | custom-call | flops 24000000000 | bytes 20000000 | tf_op jit(solution)/shard_map/pallas_call | solution.py:863
  465.9 2.5 copy.60
  468.4 1.2 slice.37
  470.3 0.7 sqrt_reduce_fusion
  471.0 0.7 sqrt.7
  471.6 0.7 slice.38
  472.4 0.6 slice.48
  472.9 0.6 fusion.1
  473.5 0.6 copy.61
  474.1 3.4 slice.52
  477.5 3.5 copy.56
  481.0 3.9 copy.57
  484.9 3.8 copy.62
  488.6 4.4 convert_element_type.30
  493.1 0.1 slice_bitcast_fusion
  493.2 0.3 copy.58
  493.5 1.3 copy.63
  494.9 5.1 fusion
  500.0 1.0 copy.67
  501.0 0.0 copy-start.1
  501.0 4.6 copy.59
  505.6 0.0 copy-start.2
  505.6 5.5 %reshape.126 = f32[2,128,4096]{2,1,0:T(8,128)} reshape(f32[2,128,8,4,128]{4,3,2,1,0:T(4,128)} %copy.59) | data formatting | bytes 8388608 | tf_op jit(solution)/shard_map/reshape | solution.py:921
  511.2 0.6 copy.72
  511.8 0.0 copy-done.2
  511.8 0.7 copy.75
  512.5 0.0 copy-done.1
  (9 shorter events, 0.1 us)
Async XLA Ops:
  0.6 5.0 copy-start
  501.0 11.5 %copy-start.1 = (bf16[2,512,1024]{2,1,0:T(8,128)(2,1)S(1)}, bf16[2,512,1024]{2,1,0:T(8,128)(2,1)}, u32[]{:S(2)}) copy-start(bf16[2,512,1024]{2,1,0:T(8,128)(2,1)} %param.20) | copy-start | bytes 6291460
  505.6 6.1 %copy-start.2 = (bf16[148,1024]{1,0:T(8,128)(2,1)S(1)}, bf16[148,1024]{1,0:T(8,128)(2,1)}, u32[]{:S(2)}) copy-start(bf16[148,1024]{1,0:T(8,128)(2,1)} %get-tuple-element.15) | copy-start | bytes 909316

commit v3 on v2

--- a/solution.py
+++ b/solution.py
@@ -236,10 +236,10 @@
     return lax.dot_general(a, b, (((ca,), (cb,)), ((), ())), preferred_element_type=F32)
 
 
-def fused_kernel(cfg, x_ref, maskrow_ref, tv_ref, small_ref, w_in, cot_ref,
-                 y_ref, gx_ref, tot_ref, o_hbm,
+def fused_kernel(cfg, x_ref, mask_ref, valid_ref, gains_ref, biases_ref, bfc_ref, cot_ref, w_qkv, w_out, w_fc1, w_fc2,
+                 y_ref, gx_ref, rms_ref, ogain_ref, obias_ref, oquery_ref, obfc_ref, o_qkv, o_out, o_fc1, o_fc2,
                  W, WO, XR, ZR, AF, QKV, OB, MF, U, H, H2, LSE,
-                 BF, PB, R0, R1, R2, DU, GW, DQKV, DO, DKV, DH, MK, MR, PS, PR, SGF, SG, SX, SZ, ST, FIN, STAT,
+                 GF, BF, PB, R0, R1, R2, DU, GW, DQKV, DO, DKV, DH, MK, MR, TV, PS, PR, SGF, SG, SX, SZ, ST, FIN, STAT,
                  loc_sem, agz_s, agz_r, agx_s, agx_r, ge_s, ge_r, re_s, re_r, wo_s, wo_r, gw_s, gw_r,
                  rx_s, rx_r, rz_s, rz_r, fo_s, fo_r, mk_s, mk_r, st_s, st_r):
     L, M, RB, T, TP, D, NC = cfg["L"], cfg["M"], cfg["RB"], cfg["T"], cfg["TP"], cfg["D"], cfg["NC"]
@@ -276,8 +276,25 @@
     def wslot(l, zz, xp, j):
         return W.at[l, zz, xp, :, COLS[j]:COLS[j + 1]]
 
-    def wsrc(l, j):
-        return w_in.at[l, :, COLS[j]:COLS[j + 1]]
+    def own_parts(l, j, s):
+        a = COLS[j]
+
+        def at_s(start, width):
+            return pl.ds(pl.multiple_of(start + width * s, width), width)
+        if j == QK:
+            return [(w_qkv.at[l, :, at_s(D * i, C)], o_qkv.at[l, :, at_s(D * i, C)], a + C * i, C) for i in range(3)]
+        if j == OUT:
+            return [(w_out.at[l, :, at_s(0, C)], o_out.at[l, :, at_s(0, C)], a, C)]
+        if j == FC1:
+            return [(w_fc1.at[l, :, at_s(S * RB * i, RB)], o_fc1.at[l, :, at_s(S * RB * i, RB)], a + RB * i, RB) for i in range(2 * M)]
+        return [(w_fc2.at[l, at_s(0, RB), :], o_fc2.at[l, at_s(0, RB), :], a, D)]
+
+    def own_load(l, j):
+        for src, _, c0, n in own_parts(l, j, s):
+            pltpu.make_async_copy(src, W.at[l, z, xx, :, c0:c0 + n], loc_sem.at[l, j]).start()
+
+    def own_wait(l, j):
+        pltpu.make_async_copy(wslot(l, z, xx, j), wslot(l, z, xx, j), loc_sem.at[l, j]).wait()
 
     def ag_pair(p, zz, xp):
         if p == 0:
@@ -286,10 +303,7 @@
         return wslot(l, zz, xp, j)
 
     def ag_own(p):
-        if p == 0:
-            return small_ref
-        l, j = divmod(p - 1, 4)
-        return wsrc(l, j)
+        return ag_pair(p, z, xx)
 
     def ag_z(p, k):
         return rcopy(ag_own(p), ag_pair(p, z, xx), agz_s.at[p, k], agz_r.at[p, z], zdev[k])
@@ -306,6 +320,8 @@
         return rcopy(ag_own(p), ag_pair(p, zz, 1 - xx), agx_s.at[p, zz], agx_r.at[p, zz], xdev)
 
     def ag_issue(p):
+        if p > 0:
+            own_wait(*divmod(p - 1, 4))
         for k in range(1, M):
             ag_z(p, k).start()
         ag_x(p, z, True).start()
@@ -337,38 +353,49 @@
         for k in range(M):
             ag_x_recv(p, zfrom[k]).wait_recv()
 
-    def ag_drain():
-        for p in range(NP):
+    def ag_drain(first, last):
+        for p in range(first, last):
             for k in range(1, M):
                 ag_z(p, k).wait_send()
             for k in range(M):
                 ag_x(p, zof[k], k == 0).wait_send()
 
-    locs = []
     for l in range(L):
-        locs.append(pltpu.make_async_copy(w_in.at[l], W.at[l, z, xx], loc_sem.at[l]))
-    ag_issue_to(1 + cfg["ahead"])
-    for c in locs:
-        c.start()
-    PS[z, xx] = small_ref[...]
-    MK[s] = maskrow_ref[...]
-    mks = [rcopy(maskrow_ref, MK.at[s], mk_s.at[i], mk_r.at[i], dev) for i, dev in enumerate((core, ydev, diag))]
+        for j in range(4):
+            own_load(l, j)
+    for l in range(L):
+        PS[z, xx, 12 * l:12 * l + 2, :] = gains_ref[l].astype(F32)
+        PS[z, xx, 12 * l + 2:12 * l + 8, :] = biases_ref[l].astype(F32)
+        for i in range(S):
+            PS[z, xx, 12 * l + 8 + i:12 * l + 9 + i, :] = bfc_ref[l:l + 1, RB * i:RB * i + RB].astype(F32)
+    row = mask_ref[...].astype(F32)
+    MK[s] = jnp.zeros_like(MK[s])
+    MK[s, 0:1, 0:T] = row
+    ag_issue_to(1)
+    mks = [rcopy(MK.at[s], MK.at[s], mk_s.at[i], mk_r.at[i], dev) for i, dev in enumerate((core, ydev, diag))]
     for c in mks:
         c.start()
+    ag_issue_to(1 + cfg["ahead"])
+    diagonal = lax.broadcasted_iota(jnp.int32, (T, T), 0) == lax.broadcasted_iota(jnp.int32, (T, T), 1)
+    TV[...] = jnp.zeros_like(TV)
+    TV[0:T, :] = jnp.broadcast_to(
+        jnp.sum(jnp.where(diagonal, row, 0.0), axis=1, keepdims=True) * valid_ref[0].astype(F32), (T, 128))
     H[0] = jnp.zeros((TP, D), F32)
     H[0, 0:T, :] = x_ref[...].astype(F32)
     SGF[...] = jnp.zeros_like(SGF)
     SG[...] = jnp.zeros_like(SG)
     STAT[...] = jnp.zeros_like(STAT)
-    for c in mks:
-        c.wait()
-    MR[...] = (MK[0] + MK[1]) + (MK[2] + MK[3])
+    for i, c in enumerate(mks):
+        c.wait_send()
+        rcopy(MK.at[s], MK.at[(core, ydev, diag)[i][1]], mk_s.at[i], mk_r.at[i], (core, ydev, diag)[i]).wait_recv()
+    MR[...] = jnp.concatenate([MK[i, :, 0:TP] for i in range(S)], axis=1)
     ag_finish(0)
     for i in range(M):
         for j in range(2):
             PR[:, 128 * (2 * i + j):128 * (2 * i + j) + 128] = PS[i, j]
-    for c in locs:
-        c.wait()
+
+    DH[...] = jnp.zeros_like(DH)
+    DH[0:T, :] = cot_ref[...].astype(F32) * TV[0:T, 0:1]
 
     def prow(l, i):
         return PR[12 * l + i:12 * l + i + 1, :]
@@ -487,7 +514,8 @@
                 outs.append(ddot(ex.astype(BF16), v, 1, 0) / tot)
                 lses.append(mx + jnp.log(tot))
             OB[l, rows, 128 * pair:128 * pair + 128] = jnp.where(lane_low, outs[0], outs[1]).astype(BF16)
-            LSE[l, pair, rows, :] = jnp.where(lane_idx == 0, lses[0], lses[1])
+            held = jnp.where(lane_idx == 2 * pair, lses[0], lses[1])
+            LSE[l, rows, :] = held if pair == 0 else jnp.where(lane_idx < 2 * pair, LSE[l, rows, :], held)
             return 0
         lax.fori_loop(0, S, block, 0)
 
@@ -500,7 +528,7 @@
             k = QKV[l, :, C + 128 * pair:C + 128 * pair + 128]
             v = QKV[l, :, 2 * C + 128 * pair:2 * C + 128 * pair + 128]
             do = DO[rows, 128 * pair:128 * pair + 128]
-            lse = LSE[l, pair, rows, :]
+            lse = LSE[l, rows, :]
             dqs = []
             dk = dv = None
             for h in range(2):
@@ -509,7 +537,7 @@
                 doh = jnp.where(keep, do, jnp.zeros_like(do))
                 sc = ddot(qh, k, 1, 1) * SCALE
                 sc = jnp.where(MR[0:1, :] > 0, sc, NEG)
-                p = jnp.exp(sc - lse[:, h:h + 1])
+                p = jnp.exp(sc - lse[:, 2 * pair + h:2 * pair + h + 1])
                 dp = ddot(doh, v, 1, 1)
                 inner = jnp.sum(p * dp, -1, keepdims=True)
                 ds = (p * (dp - inner)).astype(BF16)
@@ -561,6 +589,121 @@
         if n == 1:
             return W[l, j, :, :, a:b].reshape(2 * RB, b - a)
         return W[l, pl.ds(j * n, n), :, :, a:b].reshape(2 * RB * n, b - a)
+
+    def grad_of(l, j):
+        return GF if (l, j) == (L - 1, FC2) else W.at[l]
+
+    def GC(l, j):
+        return slice(0, D) if (l, j) == (L - 1, FC2) else slice(COLS[j], COLS[j + 1])
+
+    def rx_copy(l, j, k):
+        a, b = COLS[j], COLS[j + 1]
+        return rcopy(grad_of(l, j).at[zof[k], 1 - xx, :, GC(l, j)], XR.at[l, zof[k], :, a:b], rx_s.at[l, j, k], rx_r.at[l, j, k], xdev)
+
+    def rz_copy(l, j, k):
+        a, b = COLS[j], COLS[j + 1]
+        return rcopy(XR.at[l, zof[k], :, a:b], ZR.at[l, k - 1, :, a:b], rz_s.at[l, j, k], rz_r.at[l, j, k], zdev[k])
+
+    def rz_recv(l, j, k):
+        a, b = COLS[j], COLS[j + 1]
+        return rcopy(XR.at[l, zof[k], :, a:b], ZR.at[l, k - 1, :, a:b], rz_s.at[l, j, k], rz_r.at[l, j, k], zdev[k])
+
+    def whole_of(l, j):
+        return FIN.at[l, :, COLS[j]:COLS[j + 1]]
+
+    def fo_start(l, j):
+        for _, dst, c0, n in own_parts(l, j, s):
+            src = FIN.at[l, :, c0:c0 + n]
+            for i in range(2):
+                rcopy(src, dst, fo_s.at[l, j, i], fo_r.at[l, j, i], peers[i]).start()
+            pltpu.make_async_copy(src, dst, loc_sem.at[l, j]).start()
+
+    def fo_pass(l, j):
+        rcopy(whole_of(l, j), whole_of(l, j), fo_s.at[l, j, 1], fo_r.at[l, j, 1], peers[1]).wait_recv()
+        for _, dst, c0, n in own_parts(l, j, ydev[1]):
+            rcopy(dst, dst, fo_s.at[l, j, 2], fo_r.at[l, j, 2], core).start()
+
+    def fo_wait(l, j):
+        for i in range(3):
+            c = rcopy(whole_of(l, j), whole_of(l, j), fo_s.at[l, j, i], fo_r.at[l, j, i], peers[i])
+            c.wait_send()
+            if i != 1:
+                c.wait_recv()
+        pltpu.make_async_copy(whole_of(l, j), whole_of(l, j), loc_sem.at[l, j]).wait()
+
+    def red_first(l, j, k):
+        a, b = COLS[j], COLS[j + 1]
+        rx_copy(l, j, k).wait_recv()
+        zz = zof[k]
+        if k == 0:
+            return
+        for r0 in range(0, RB, 32):
+            XR[l, zz, r0:r0 + 32, a:b] = (XR[l, zz, r0:r0 + 32, a:b].astype(F32) + grad_of(l, j)[zz, xx, r0:r0 + 32, GC(l, j)].astype(F32)).astype(BF16)
+        rz_copy(l, j, k).start()
+
+    def red_second(l, j):
+        a, b = COLS[j], COLS[j + 1]
+        red_first(l, j, 0)
+        for k in range(1, M):
+            rz_recv(l, j, k).wait_recv()
+        for r0 in range(0, RB, 32):
+            t = XR[l, z, r0:r0 + 32, a:b].astype(F32) + grad_of(l, j)[z, xx, r0:r0 + 32, GC(l, j)].astype(F32)
+            for k in range(1, M):
+                t = t + ZR[l, k - 1, r0:r0 + 32, a:b].astype(F32)
+            FIN[l, r0:r0 + 32, a:b] = t.astype(BF16)
+        fo_start(l, j)
+
+    def red_end(l, j):
+        for k in range(M):
+            rx_copy(l, j, k).wait_send()
+        for k in range(1, M):
+            rz_copy(l, j, k).wait_send()
+        fo_wait(l, j)
+
+    events = []
+    later = []
+    done = {"n": 0}
+
+    def red_later():
+        if len(later) > 1:
+            events.append((fo_pass,) + later.pop(0))
+        if later:
+            events.append((red_second,) + later[-1])
+
+    def red_push(l, j):
+        for k in list(range(1, M)) + [0]:
+            rx_copy(l, j, k).start()
+        events.extend((red_first, l, j, k) for k in range(1, M))
+        red_later()
+        later.append((l, j))
+
+    def red_service(n):
+        for _ in range(n):
+            if done["n"] >= len(events):
+                return
+            f, *a = events[done["n"]]
+            done["n"] += 1
+            f(*a)
+
+    def norm_back(l, src, e, gain):
+        def one(rows, acc):
+            n, r = norm(src[l, rows, :])
+            dm = re_rows(e, rows)
+            dn = dm * gain
+            pm = jnp.mean(dn, -1, keepdims=True)
+            cm = jnp.mean(dn * n, -1, keepdims=True)
+            DH[rows, :] = DH[rows, :] + r * (dn - pm - n * cm)
+            return acc[0] + fold(dm * n), acc[1] + fold(dm)
+        zero = jnp.zeros((8, D), F32)
+        g, b = row_loop(one, (zero, zero))
+        return col_sum(g), col_sum(b)
+
+    def low_of(buf):
+        def one(rows, acc):
+            v = DH[rows, :].astype(BF16)
+            buf[s, rows, :] = v
+            return acc + fold(v.astype(F32))
+        return col_sum(row_loop(one, jnp.zeros((8, D), F32)))
 
     def forward(l):
         e = 2 * l
@@ -583,10 +726,15 @@
             QKV[l, :, C * n:C * n + C] = r.astype(BF16)
         ag_finish(1 + 4 * l + OUT)
         wo_start(l)
+        if l == 0:
+            SGF[12 * (L - 1) + 7:12 * (L - 1) + 8, :] = low_of(BF.at[0])
+            ge_start(2 * L, BF.at[0])
         attend(l, 0)
         ag_service(1)
         attend(l, 1)
         ag_service(1)
+        if l == 0:
+            ge_end(2 * L, BF.at[0])
         wo_end(l)
         re_run(e + 0, partial_of(
             lambda chip: OB[l, pl.ds(pl.multiple_of(chip * 2 * TP, 16), 2 * TP), :],
@@ -601,7 +749,7 @@
             H2[l, rows, :] = mid
             n, _r = norm(mid)
             MF[l, s, rows, :] = (n * prow(l, 1) + prow(l, 6)).astype(BF16)
-            t = tv_ref[rows, 0:1]
+            t = TV[rows, 0:1]
             return acc[0] + fold(t * hv * hv), acc[1] + fold(t * br * br)
         zero = jnp.zeros((8, D), F32)
         s0, s1 = row_loop(post, (zero, zero))
@@ -615,166 +763,84 @@
             u = u + bias[:, C * j:C * j + C]
             U[l, :, C * j:C * j + C] = u
             GW[:, C * j:C * j + C] = (u / (1.0 + jnp.exp(-1.702 * u))).astype(BF16)
+        stat(3 * l, s0)
+        stat(3 * l + 1, s1)
+        if l == L - 1:
+            for j in range(FS // C):
+                GF[j, :, :, :] = ddot(GW[:, C * j:C * j + C], BF[0].reshape(R, D), 0, 0).astype(BF16).reshape(2, RB, D)
         ag_finish(1 + 4 * l + FC2)
+        if l == L - 1:
+            red_push(l, FC2)
         re_run(e + 1, partial_of(
             lambda chip: GW[pl.ds(pl.multiple_of(chip * 2 * TP, 16), 2 * TP), :],
             lambda j: W[l, :, :, :, pl.ds(pl.multiple_of(COLS[FC2] + j * C, C), C)].reshape(FS, C), 0))
-        ag_service(2)
-        re_end(e + 1)
+
+    def forward_end(l):
+        e = 2 * l
 
         def last(rows, acc):
             out = re_rows(e + 1, rows) + prow(l, 7)
             res = H2[l, rows, :] + out
             H[l + 1, rows, :] = res
-            t = tv_ref[rows, 0:1]
+            t = TV[rows, 0:1]
             return acc + fold(t * out * out)
-        s2 = row_loop(last, zero)
-        for i, v in enumerate((s0, s1, s2)):
-            STAT[...] = jnp.where(lane_idx == 3 * l + i, jnp.sum(col_sum(v), axis=1, keepdims=True), STAT[...])
-
-    for l in range(L):
-        forward(l)
-    STAT[...] = jnp.where(lane_idx == 3 * L, col_sum(tv_ref[:, 0:1]), STAT[...])
-    y_ref[...] = H[L, 0:T, :].astype(BF16)
-    ag_drain()
-
-    def rx_copy(l, j):
-        a, b = COLS[j], COLS[j + 1]
-        return rcopy(W.at[l, :, 1 - xx, :, a:b], XR.at[l, :, :, a:b], rx_s.at[l, j], rx_r.at[l, j], xdev)
-
-    def rz_copy(l, j, k):
-        a, b = COLS[j], COLS[j + 1]
-        return rcopy(XR.at[l, zof[k], :, a:b], ZR.at[l, z, :, a:b], rz_s.at[l, j, k], rz_r.at[l, j, k], zdev[k])
-
-    def rz_recv(l, j, k):
-        a, b = COLS[j], COLS[j + 1]
-        return rcopy(XR.at[l, zof[k], :, a:b], ZR.at[l, zfrom[k], :, a:b], rz_s.at[l, j, k], rz_r.at[l, j, k], zdev[k])
-
-    def fo_copy(l, j, i):
-        a, b = COLS[j], COLS[j + 1]
-        return rcopy(FIN.at[l, :, a:b], o_hbm.at[l, s, :, a:b], fo_s.at[l, j, i], fo_r.at[l, j, i], peers[i])
-
-    def fo_recv(l, j, i):
-        a, b = COLS[j], COLS[j + 1]
-        return rcopy(FIN.at[l, :, a:b], o_hbm.at[l, peers[i][1], :, a:b], fo_s.at[l, j, i], fo_r.at[l, j, i], peers[i])
-
-    def fo_local(l, j):
-        a, b = COLS[j], COLS[j + 1]
-        return pltpu.make_async_copy(FIN.at[l, :, a:b], o_hbm.at[l, s, :, a:b], loc_sem.at[L + 4 * l + j])
-
-    def red_first(l, j):
-        a, b = COLS[j], COLS[j + 1]
-        rx_copy(l, j).wait_recv()
-        for k in list(range(1, M)) + [0]:
-            zz = zof[k]
-            for r0 in range(0, RB, 32):
-                XR[l, zz, r0:r0 + 32, a:b] = (XR[l, zz, r0:r0 + 32, a:b].astype(F32) + W[l, zz, xx, r0:r0 + 32, a:b].astype(F32)).astype(BF16)
-            if k > 0:
-                rz_copy(l, j, k).start()
-
-    def red_second(l, j):
-        a, b = COLS[j], COLS[j + 1]
-        for k in range(1, M):
-            rz_recv(l, j, k).wait_recv()
-        for r0 in range(0, RB, 32):
-            t = XR[l, z, r0:r0 + 32, a:b].astype(F32)
-            for k in range(1, M):
-                t = t + ZR[l, zfrom[k], r0:r0 + 32, a:b].astype(F32)
-            FIN[l, r0:r0 + 32, a:b] = t.astype(BF16)
-        for i in range(3):
-            fo_copy(l, j, i).start()
-        fo_local(l, j).start()
-
-    def red_end(l, j):
-        rx_copy(l, j).wait_send()
-        for k in range(1, M):
-            rz_copy(l, j, k).wait_send()
-        for i in range(3):
-            fo_copy(l, j, i).wait_send()
-            fo_recv(l, j, i).wait_recv()
-        fo_local(l, j).wait()
-
-    events = []
-    done = {"n": 0}
-
-    def red_push(l, j):
-        rx_copy(l, j).start()
-        events.append((red_first, l, j))
-
-    def red_service(n):
-        for _ in range(n):
-            if done["n"] >= len(events):
-                return
-            f, l, j = events[done["n"]]
-            done["n"] += 1
-            f(l, j)
-            if f is red_first:
-                events.insert(min(done["n"] + 1, len(events)), (red_second, l, j))
-
-    def norm_back(l, src, e, gain):
-        def one(rows, acc):
-            n, r = norm(src[l, rows, :])
-            dm = re_rows(e, rows)
-            dn = dm * gain
-            pm = jnp.mean(dn, -1, keepdims=True)
-            cm = jnp.mean(dn * n, -1, keepdims=True)
-            DH[rows, :] = DH[rows, :] + r * (dn - pm - n * cm)
-            return acc[0] + fold(dm * n), acc[1] + fold(dm)
-        zero = jnp.zeros((8, D), F32)
-        g, b = row_loop(one, (zero, zero))
-        return col_sum(g), col_sum(b)
-
-    def low_of(buf):
-        def one(rows, acc):
-            v = DH[rows, :].astype(BF16)
-            buf[s, rows, :] = v
-            return acc + fold(v.astype(F32))
-        return col_sum(row_loop(one, jnp.zeros((8, D), F32)))
+        re_end(e + 1)
+        stat(3 * l + 2, row_loop(last, jnp.zeros((8, D), F32)))
+
+    def stat(i, v):
+        STAT[...] = jnp.where(lane_idx == i, jnp.sum(col_sum(v), axis=1, keepdims=True), STAT[...])
 
     def backward(l):
         ge_a = re_a = 2 * L + 2 * (L - 1 - l)
         ge_b = re_b = ge_a + 1
         B0, B1 = BF.at[0], BF.at[1]
-        SGF[12 * l + 7:12 * l + 8, :] = low_of(B0)
-        ge_start(ge_a, B0)
-        red_service(1)
-        ge_end(ge_a, B0)
+        svc = cfg["svc"][L - 1 - l]
+        if l < L - 1:
+            SGF[12 * l + 7:12 * l + 8, :] = low_of(B0)
+            ge_start(ge_a, B0)
+            red_service(svc[0])
+            ge_end(ge_a, B0)
         for j in range(FS // C):
             dg = ddot(BF[0].reshape(R, D), wtile(l, j, COLS[FC2], COLS[FC2] + D), 1, 1)
             u = U[l, :, C * j:C * j + C]
             sg = 1.0 / (1.0 + jnp.exp(-1.702 * u))
-            GW[:, C * j:C * j + C] = (u * sg).astype(BF16)
+            if l < L - 1:
+                GW[:, C * j:C * j + C] = (u * sg).astype(BF16)
             du = (dg * (sg + 1.702 * u * sg * (1.0 - sg))).astype(BF16)
             DU[:, C * j:C * j + C] = du
             SGF[pl.ds(12 * l + 8 + s, 1), C * j:C * j + C] = jnp.sum(du.astype(F32), axis=0, keepdims=True)
-        red_service(1)
-        for j in range(FS // C):
-            W[l, j, :, :, COLS[FC2]:COLS[FC2] + D] = ddot(GW[:, C * j:C * j + C], BF[0].reshape(R, D), 0, 0).astype(BF16).reshape(2, RB, D)
-        red_push(l, FC2)
+        red_service(svc[1])
+        if l < L - 1:
+            for j in range(FS // C):
+                W[l, j, :, :, COLS[FC2]:COLS[FC2] + D] = ddot(GW[:, C * j:C * j + C], BF[0].reshape(R, D), 0, 0).astype(BF16).reshape(2, RB, D)
+            red_push(l, FC2)
         re_run(re_a, partial_of(
             lambda chip: DU[pl.ds(pl.multiple_of(chip * 2 * TP, 16), 2 * TP), :],
             lambda j: wtile(l, j, COLS[FC1], COLS[FC1] + FS), 1))
         for j in range(S):
             W[l, j, :, :, COLS[FC1]:COLS[FC1] + FS] = ddot(MF[l, :, :, C * j:C * j + C].reshape(R, C), DU[...], 0, 0).astype(BF16).reshape(2, RB, FS)
         red_push(l, FC1)
+        if l == L - 1:
+            forward_end(l)
+        red_service(svc[2])
         re_end(re_a)
         gg, bb = norm_back(l, H2, re_a, prow(l, 1))
         SGF[12 * l + 1:12 * l + 2, :] = gg
         SGF[12 * l + 6:12 * l + 7, :] = bb
         SGF[12 * l + 5:12 * l + 6, :] = low_of(B1)
         ge_start(ge_b, B1)
-        red_service(1)
+        red_service(svc[3])
         ge_end(ge_b, B1)
         DO[...] = ddot(BF[1].reshape(R, D), WO[l].reshape(C, D), 1, 1).astype(BF16)
         for j in range(S):
             WO[l, :, :, C * j:C * j + C] = ddot(OB[l], BF[1, :, :, C * j:C * j + C].reshape(R, C), 0, 0).astype(BF16).reshape(2, RB, C)
         gw_start(l)
         attend_back(l, 0)
-        red_service(1)
+        red_service(svc[4])
         attend_back(l, 1)
         gw_end(l)
         red_push(l, OUT)
-        red_service(1)
+        red_service(svc[5])
         for i, (row, c0) in enumerate(((3, 0), (4, 2 * C))):
             SGF[12 * l + row:12 * l + row + 1, pl.ds(pl.multiple_of(C * s, C), C)] = jnp.sum(
                 DQKV[:, c0:c0 + C].astype(F32), axis=0, keepdims=True)
@@ -784,16 +850,23 @@
         for j in range(S):
             W[l, j, :, :, 0:3 * C] = ddot(AF[l, :, :, C * j:C * j + C].reshape(R, C), DQKV[...], 0, 0).astype(BF16).reshape(2, RB, 3 * C)
         red_push(l, QK)
+        red_service(svc[6])
         re_end(re_b)
         gg, bb = norm_back(l, H, re_b, prow(l, 0))
         SGF[12 * l + 0:12 * l + 1, :] = gg
         SGF[12 * l + 2:12 * l + 3, :] = bb
-
-    DH[...] = jnp.zeros_like(DH)
-    DH[0:T, :] = cot_ref[...].astype(F32) * tv_ref[0:T, 0:1]
+        red_service(svc[7])
+
+    for l in range(L):
+        forward(l)
+        if l < L - 1:
+            forward_end(l)
+    ag_drain(0, NP - 1)
     for l in reversed(range(L)):
         backward(l)
     gx_ref[...] = DH[0:T, :]
+    y_ref[...] = H[L, 0:T, :].astype(BF16)
+    STAT[...] = jnp.where(lane_idx == 3 * L, col_sum(TV[:, 0:1]), STAT[...])
 
     for i in range(M):
         for j in range(2):
@@ -801,36 +874,51 @@
             SG[i, j, 24:25, :] = STAT[...]
     sgx = rcopy(SG.at[:, 1 - xx], SX, st_s.at[0], st_r.at[0], xdev)
     sgx.start()
+
+    def sz(k, frm):
+        return rcopy(SX.at[zof[k]], SZ.at[zfrom[k] if frm else z], st_s.at[k], st_r.at[k], zdev[k])
+
+    def stc(i, frm):
+        slot = peers[i][1] if frm else s
+        return rcopy(ST.at[s], ST.at[slot], st_s.at[M + i], st_r.at[M + i], peers[i])
+
+    red_service(len(events))
     sgx.wait()
     SX[...] = SX[...] + SG[:, xx]
     SZ[z] = SX[z]
-
-    def sz(k, frm):
-        return rcopy(SX.at[zof[k]], SZ.at[zfrom[k] if frm else z], st_s.at[k], st_r.at[k], zdev[k])
     for k in range(1, M):
         sz(k, False).start()
-    red_service(2)
+    red_later()
+    red_service(len(events))
     for k in range(1, M):
         sz(k, True).wait_recv()
     tot = SZ[0]
     for k in range(1, M):
         tot = tot + SZ[k]
     ST[s] = tot
-
-    def stc(i, frm):
-        slot = peers[i][1] if frm else s
-        return rcopy(ST.at[s], ST.at[slot], st_s.at[M + i], st_r.at[M + i], peers[i])
     for i in range(3):
         stc(i, False).start()
-    while done["n"] < len(events):
-        red_service(1)
+    for p in later:
+        fo_pass(*p)
     for i in range(3):
         stc(i, True).wait_recv()
-    tot_ref[...] = (ST[0] + ST[1]) + (ST[2] + ST[3])
+    tot = (ST[0] + ST[1]) + (ST[2] + ST[3])
+    for l in range(L):
+        ogain_ref[l] = tot[12 * l:12 * l + 2]
+        obias_ref[l, 0:1, :] = tot[12 * l + 2:12 * l + 3]
+        obias_ref[l, 1:5, :] = tot[12 * l + 4:12 * l + 8]
+        oquery_ref[l:l + 1, :] = tot[12 * l + 3:12 * l + 4]
+        for i in range(S):
+            obfc_ref[l:l + 1, RB * i:RB * i + RB] = tot[12 * l + 8 + i:12 * l + 9 + i]
+    sums = tot[12 * L:12 * L + 1]
+    root = jnp.sqrt(sums / (jnp.maximum(sums[:, 3 * L:3 * L + 1], 1.0) * D))
+    for l in range(L):
+        rms_ref[l:l + 1, :] = root[:, 3 * l:3 * l + 3]
     for k in range(1, M):
         sz(k, False).wait_send()
     for i in range(3):
         stc(i, False).wait_send()
+    ag_drain(NP - 1, NP)
     for l in reversed(range(L)):
         for j in (FC2, FC1, OUT, QK):
             red_end(l, j)
@@ -839,42 +927,35 @@
 def fused_local(cfg, block_input, key_mask, valid, gains, biases, w_qkv, w_out, w_fc1, b_fc1, w_fc2, cotangent):
     L, M, RB, T, TP, D, NC, FS = (cfg[n] for n in ("L", "M", "RB", "T", "TP", "D", "NC", "FS"))
     S, dp = 4, 2 * M
-    me = lax.axis_index("seq")
     C = D // S
     R = S * TP
-
-    def columns(w, outer):
-        view = w.reshape(L, RB, outer, S, -1)
-        return lax.dynamic_index_in_dim(view, me, 3, False).reshape(L, RB, -1)
-
-    w_in = jnp.concatenate([
-        columns(w_qkv, 3), columns(w_out, 1), columns(w_fc1, dp),
-        lax.dynamic_index_in_dim(w_fc2.reshape(L, S, RB, D), me, 1, False)], 2)
-    small = jnp.concatenate([gains, biases, b_fc1.reshape(L, S, -1)], 1).astype(F32).reshape(L * 12, RB)
-    mask = jnp.pad(key_mask[0].astype(F32), (0, TP - T))
-    mask_row = jnp.where(jnp.arange(S)[:, None] == me, mask[None, :], 0.0).reshape(1, R)
-    mask_row = jnp.broadcast_to(mask_row, (8, R))
-    tv = jnp.broadcast_to((mask * valid[0].astype(F32))[:, None], (TP, 128))
     vm = pl.BlockSpec(memory_space=pltpu.VMEM)
     hbm = pl.BlockSpec(memory_space=pl.ANY)
     dma = pltpu.SemaphoreType.DMA
     v = pltpu.VMEM
     NP, NE = 1 + 4 * L, 4 * L
-    y, gx, tot, og = pl.pallas_call(
+    out = pl.pallas_call(
         partial(fused_kernel, cfg),
         out_shape=(
             jax.ShapeDtypeStruct((T, D), BF16),
             jax.ShapeDtypeStruct((T, D), F32),
-            jax.ShapeDtypeStruct((32, RB), F32),
-            jax.ShapeDtypeStruct((L, S, RB, NC), BF16),
+            jax.ShapeDtypeStruct((L, 3), F32),
+            jax.ShapeDtypeStruct((L, 2, RB), F32),
+            jax.ShapeDtypeStruct((L, 5, RB), F32),
+            jax.ShapeDtypeStruct((L, RB), F32),
+            jax.ShapeDtypeStruct((L, S * RB), F32),
+            jax.ShapeDtypeStruct(w_qkv.shape, BF16),
+            jax.ShapeDtypeStruct(w_out.shape, BF16),
+            jax.ShapeDtypeStruct(w_fc1.shape, BF16),
+            jax.ShapeDtypeStruct(w_fc2.shape, BF16),
         ),
-        in_specs=[vm, vm, vm, vm, hbm, vm],
-        out_specs=(vm, vm, vm, hbm),
+        in_specs=[vm, vm, pl.BlockSpec(memory_space=pltpu.SMEM), vm, vm, vm, vm, hbm, hbm, hbm, hbm],
+        out_specs=(vm,) * 7 + (hbm,) * 4,
         scratch_shapes=[
             v((L, M, 2, RB, NC), BF16),
             v((L, 2, RB, D), BF16),
             v((L, M, RB, NC), BF16),
-            v((L, M, RB, NC), BF16),
+            v((L, M - 1, RB, NC), BF16),
             v((L, S, TP, D), BF16),
             v((L, R, 3 * C), BF16),
             v((L, R, C), BF16),
@@ -882,7 +963,8 @@
             v((L, R, FS), F32),
             v((L + 1, TP, D), F32),
             v((L, TP, D), F32),
-            v((L, 2, R, 128), F32),
+            v((L, R, 128), F32),
+            v((M, 2, RB, D), BF16),
             v((2, S, TP, D), BF16),
             v((2, 2, 2, TP, D), BF16),
             v((2, TP, D), BF16),
@@ -894,8 +976,9 @@
             v((R, C), BF16),
             v((2, R, 128), F32),
             v((TP, D), F32),
-            v((S, 8, R), F32),
+            v((S, 8, -(-TP // 128) * 128), F32),
             v((8, R), F32),
+            v((TP, 128), F32),
             v((M, 2, 12 * L, RB), F32),
             v((12 * L, D), F32),
             v((12 * L, D), F32),
@@ -905,35 +988,20 @@
             v((S, 32, RB), F32),
             v((L, RB, NC), BF16),
             v((1, RB), F32),
-            dma((5 * L,)),
+            dma((L, 4)),
             dma((NP, M)), dma((NP, M)), dma((NP, M)), dma((NP, M)),
             dma((NE, 3, 2)), dma((NE, 3, 2)), dma((NE, 3)), dma((NE, 3)),
             dma((L, 3)), dma((L, 3)), dma((L, 3)), dma((L, 3)),
-            dma((L, 4)), dma((L, 4)), dma((L, 4, M)), dma((L, 4, M)),
+            dma((L, 4, M)), dma((L, 4, M)), dma((L, 4, M)), dma((L, 4, M)),
             dma((L, 4, 3)), dma((L, 4, 3)), dma((3,)), dma((3,)), dma((M + 3,)), dma((M + 3,)),
         ],
         compiler_params=pltpu.CompilerParams(
             collective_id=0, has_side_effects=True, vmem_limit_bytes=cfg["vmem"]),
         cost_estimate=pl.CostEstimate(flops=24_000_000_000, bytes_accessed=20_000_000, transcendentals=0),
-    )(block_input[0], mask_row, tv, small, w_in, cotangent[0])
-    g = og.astype(F32)
-    parts = (g[..., :3 * C], g[..., 3 * C:4 * C], g[..., 4 * C:4 * C + FS], g[..., 4 * C + FS:])
-    join = lambda a, outer: a.reshape(L, S, RB, outer, -1).transpose(0, 2, 3, 1, 4).reshape(L, RB, -1)
-    rows = tot[:12 * L].reshape(L, 12, RB)
-    rms = jnp.sqrt(tot[24, :3 * L].reshape(L, 3) / (jnp.maximum(tot[24, 3 * L], 1.0) * D))
-    return (
-        y[None],
-        gx[None],
-        rms,
-        rows[:, :2],
-        jnp.concatenate([rows[:, 2:3], rows[:, 4:8]], 1),
-        rows[:, 3],
-        join(parts[0], 3),
-        join(parts[1], 1),
-        join(parts[2], dp),
-        rows[:, 8:12].reshape(L, S * RB),
-        parts[3].reshape(L, S * RB, D),
-    )
+    )(block_input[0], key_mask, valid, gains, biases, b_fc1, cotangent[0], w_qkv, w_out, w_fc1, w_fc2)
+    y, gx, rms, o_gain, o_bias, o_query, o_bfc, o_qkv, o_out, o_fc1, o_fc2 = out
+    return (y[None], gx[None], rms, o_gain, o_bias, o_query,
+            o_qkv.astype(F32), o_out.astype(F32), o_fc1.astype(F32), o_bfc, o_fc2.astype(F32))
 
 
 def local(*args):
@@ -946,7 +1014,8 @@
             and FS // dp == RB and HEAD_DIM * 2 == 128 and D // S == 4 * HEAD_DIM and block_input.shape[0] == 1)
     if not fits:
         return plain_local(*args)
-    cfg = dict(L=L, M=dp // 2, RB=RB, T=T, TP=-(-T // 16) * 16, D=D, NC=D + 2 * FS, FS=FS, ahead=2, vmem=60 * 2**20)
+    cfg = dict(L=L, M=dp // 2, RB=RB, T=T, TP=-(-T // 16) * 16, D=D, NC=D + 2 * FS, FS=FS, ahead=2, vmem=62 * 2**20,
+               svc=((0, 0, 2, 1, 0, 1, 2, 0),) + ((8, 3, 2, 3, 1, 1, 3, 0),) * (L - 1))
     return fused_local(cfg, *args)
 
 

time: 522 us -> 382 us (0.73)
  the two profiles are of different devices: /device:TPU:23 before, /device:TPU:9 now
where the time goes in v3:
time: 382 us; the launch traced here: 375 us
  Pallas kernels  357 us (93%)
  other arithmetic  9.83 us (3%)
  local copies, waits for them, and re-layouts  6.37 us (2%)
    pallas_call x1, Pallas kernels, fused_local(): pl.pallas_call(partial(fused_kernel, cfg), out_shape=(jax.ShapeDtypeStruc...  357 us

profile of v3, /device:TPU:9, one launch (start us, length us, event | category | flops | bytes accessed | tf_op | source)
XLA Modules:
  0.0 374.8 jit_solution(6473619120500271669)
XLA Ops:
  0.6 1.3 copy.22.biases_ref
  2.6 356.8 %shard_map.194 = (bf16[148,1024]{1,0:T(8,128)(2,1)}, f32[148,1024]{1,0:T(8,128)}, f32[2,3]{1,0:T(2,128)}, f32[2,2,128]{2,1,0:T(2,128)}, f32[2,5,128]{2,1,0:T(8,1...) custom-call(bf16[148,1024]{1,0:T(8,128)(2,1)} %bitcast.6, ...), custom_call_target="tpu_custom_call" | custom-call | flops 24000000000 | bytes 20000000 | tf_op jit(solution)/shard_map/pallas_call | solution.py:937
  359.4 0.0 copy-start
  359.4 4.2 %convert_element_type.14 = f32[2,128,4096]{2,1,0:T(8,128)} convert(bf16[2,128,4096]{2,1,0:T(8,128)(2,1)} %get-tuple-element.30) | non-fusion elementwise | flops 1048576 | bytes 6291456 | tf_op jit(solution)/shard_map/convert_element_type | solution.py:1004
  363.7 0.0 copy-done
  363.7 0.0 copy-start.1
  363.7 2.5 convert_element_type.15
  366.1 0.0 copy-done.1
  366.2 0.0 copy-start.3
  366.2 0.0 copy-start.2
  366.2 2.0 convert_element_type.12
  368.2 0.0 copy-start.5
  368.2 0.0 copy-start.4
  368.2 0.0 copy-start.9
  368.2 0.0 copy-start.7
  368.2 0.0 copy-start.8
  368.2 0.0 copy-start.6
  368.2 0.0 copy-done.3
  368.2 1.1 convert_element_type.13
  369.3 0.0 copy-done.2
  369.3 1.4 copy.23
  370.8 0.0 copy-done.5
  370.8 0.6 copy.24
  371.4 0.0 copy-done.4
  371.4 0.7 copy.31
  372.1 0.0 copy-done.9
  372.1 0.6 copy.32
  372.6 0.0 copy-done.7
  372.6 0.6 copy.33
  373.2 0.0 copy-done.8
  373.2 0.6 copy.34
  373.8 0.0 copy-done.6
  373.8 0.6 copy.35
Async XLA Ops:
  359.4 4.3 %copy-start = (bf16[2,512,1024]{2,1,0:T(8,128)(2,1)S(1)}, bf16[2,512,1024]{2,1,0:T(8,128)(2,1)}, u32[]{:S(2)}) copy-start(bf16[2,512,1024]{2,1,0:T(8,128)(2,1)} %get-tuple-element.32) | copy-start | bytes 6291460
  363.7 2.5 copy-start.1
  366.2 2.1 copy-start.3
  366.2 3.2 copy-start.2
  368.2 2.6 copy-start.5
  368.2 3.2 copy-start.4
  368.2 3.9 %copy-start.9 = (f32[2,3]{1,0:T(2,128)S(1)}, f32[2,3]{1,0:T(2,128)}, u32[]{:S(2)}) copy-start(f32[2,3]{1,0:T(2,128)} %get-tuple-element.57) | copy-start | bytes 76
  368.2 4.5 %copy-start.7 = (f32[2,2,128]{2,1,0:T(2,128)S(1)}, f32[2,2,128]{2,1,0:T(2,128)}, u32[]{:S(2)}) copy-start(f32[2,2,128]{2,1,0:T(2,128)} %get-tuple-element.58) | copy-start | bytes 6148
  368.2 5.0 %copy-start.8 = (f32[2,128]{1,0:T(2,128)S(1)}, f32[2,128]{1,0:T(2,128)}, u32[]{:S(2)}) copy-start(f32[2,128]{1,0:T(2,128)} %get-tuple-element.60) | copy-start | bytes 3076
  368.2 5.6 %copy-start.6 = (f32[2,512]{1,0:T(2,128)S(1)}, f32[2,512]{1,0:T(2,128)}, u32[]{:S(2)}) copy-start(f32[2,512]{1,0:T(2,128)} %get-tuple-element.64) | copy-start | bytes 12292
